TPU v7x, 256 devices: a whole 4x4x8 slice. The times are simulated.
256 devices in a mesh: leaf: 32 (over z, y), front: 8 (over x, core).
Axes of the slice: x: 4, y: 4, z: 8, core: 2. Of those that a mesh axis runs over, the one named last changes fastest.
Arguments:
- rhs_sub: float32 [131072, 64], P(('leaf', 'front')), may hold values from -6 to 6
- rhs_root: float32 [12288, 64], P(('leaf', 'front')), may hold values from -6 to 6
- factor_sub: bfloat16 [32, 4096, 4096], P('leaf', 'front'), may hold values from -0.09375 to 0.09375
- coupling: bfloat16 [32, 2048, 4096], P('leaf', None, 'front'), may hold values from -0.09375 to 0.09375
- update_rows: int32 [32, 2048], P('leaf'), may hold values from 0 to 12287, as said below
- factor_root: bfloat16 [12288, 12288], P(('leaf', 'front')), may hold values from -0.0546875 to 0.0546875
- mass_sub: float32 [131072], P(('leaf', 'front')), may hold values from 0.5 to 2
- mass_root: float32 [12288], P(('leaf', 'front')), may hold values from 0.5 to 2
- interface: bfloat16 [256, 256, 256], P(('leaf', 'front')), may hold values from -0.375 to 0.375
- basis_sub: bfloat16 [131072, 2048], P(('leaf', 'front')), may hold values from -0.046875 to 0.046875
- basis_root: bfloat16 [12288, 2048], P(('leaf', 'front')), may hold values from -0.046875 to 0.046875
Outputs:
- new_sub: float32 [131072, 64], P(('leaf', 'front'))
- new_root: float32 [12288, 64], P(('leaf', 'front'))
- gram: float32 [2048, 64], replicated
Inputs may be any that keep to these rules, and one draw needn't show every extreme that they name: Each row of update_rows lists 2048 distinct root rows.
All inputs are finite; a program needn't handle non-finite values.
Results may differ from a plain program's by a relative error of at most 0.015.
Values may be sent and summed in bfloat16 or wider, within the bound.
A program may use at most 128 MiB of HBM per device.

v0:
```python
import jax
import jax.numpy as jnp
from jax import lax
from jax.sharding import PartitionSpec as P


def shifted(block, axis, distance):
    devices = range(lax.axis_size(axis))
    route = [((i - distance) % len(devices), i) for i in devices]
    return lax.ppermute(block, axis, route)


def contract_first(left, right):
    return lax.dot_general(
        left, right, (((0,), (0,)), ((), ())), preferred_element_type=jnp.float32
    )


def body(
    rhs_sub,
    rhs_root,
    factor_sub,
    coupling,
    update_rows,
    factor_root,
    mass_sub,
    mass_root,
    interface,
    basis_sub,
    basis_root,
):
    row_count = rhs_sub.shape[0]
    width = rhs_sub.shape[1]
    front_pos = lax.axis_index("front")
    flat_pos = lax.axis_index(("leaf", "front"))
    row_base = front_pos * row_count
    my_factor = factor_sub[0]
    zero_low = jnp.zeros((), jnp.bfloat16)
    rhs_low = rhs_sub.astype(jnp.bfloat16)
    block_rows = lax.all_gather(rhs_low, "front", axis=0, tiled=True)
    count = block_rows.shape[0]
    columns = my_factor
    row_ids = row_base + lax.broadcasted_iota(jnp.int32, (row_count, count), 0)
    col_ids = lax.broadcasted_iota(jnp.int32, (row_count, count), 1)
    columns = jnp.where(col_ids <= row_ids, columns, zero_low)
    y_mine = jnp.dot(columns, block_rows, preferred_element_type=jnp.float32)
    y_low = y_mine.astype(jnp.bfloat16)
    update_term = jnp.dot(coupling[0], y_low, preferred_element_type=jnp.float32)
    root_rows = factor_root.shape[0]
    root_order = factor_root.shape[1]
    root_base = flat_pos * root_rows
    root_ids = root_base + lax.broadcasted_iota(jnp.int32, (root_rows, root_order), 0)
    root_cols = lax.broadcasted_iota(jnp.int32, (root_rows, root_order), 1)
    masked_root = jnp.where(root_cols <= root_ids, factor_root, zero_low)
    scattered = jnp.zeros((root_order, width), jnp.float32).at[update_rows[0]].add(update_term)
    own_part = lax.dynamic_slice_in_dim(scattered, root_base, root_rows, 0) - rhs_root
    scattered = lax.dynamic_update_slice_in_dim(scattered, own_part, root_base, 0)
    root_mine = -lax.psum_scatter(scattered, ("leaf", "front"), scatter_dimension=0, tiled=True)
    columns = masked_root
    y_root = jnp.dot(
        columns,
        lax.all_gather(root_mine.astype(jnp.bfloat16), ("leaf", "front"), axis=0, tiled=True),
        preferred_element_type=jnp.float32,
    )
    back_partial = contract_first(masked_root, y_root.astype(jnp.bfloat16))
    x_full = lax.psum(back_partial, ("leaf", "front"))
    x_root = lax.dynamic_slice_in_dim(x_full, root_base, root_rows, 0)
    x_full_low = x_full.astype(jnp.bfloat16)
    picked = jnp.take(x_full_low, update_rows[0], axis=0)
    t_low = (y_mine - contract_first(coupling[0], picked)).astype(jnp.bfloat16)
    columns = my_factor
    row_ids = row_base + lax.broadcasted_iota(
        jnp.int32, (row_count, row_count * lax.axis_size("front")), 0
    )
    col_ids = lax.broadcasted_iota(jnp.int32, (row_count, row_count * lax.axis_size("front")), 1)
    columns = jnp.where(col_ids <= row_ids, columns, zero_low)
    x_sub = lax.psum_scatter(
        contract_first(columns, t_low), "front", scatter_dimension=0, tiled=True
    )
    x_low = x_sub.astype(jnp.bfloat16)
    rim_size = interface.shape[1]
    from_prev = shifted(x_low[row_count - rim_size :], "leaf", 1)
    first_add = jnp.dot(interface[0], from_prev, preferred_element_type=jnp.float32)
    back_send = contract_first(interface[0], x_low[:rim_size])
    from_next = shifted(back_send.astype(jnp.bfloat16), "leaf", -1).astype(back_send.dtype)
    mass_x = mass_sub[:, None] * x_sub
    mass_x = mass_x.at[:rim_size].add(first_add)
    mass_x = mass_x.at[row_count - rim_size :].add(from_next)
    mass_root_x = mass_root[:, None] * x_root
    gram_part = contract_first(basis_sub, mass_x.astype(jnp.bfloat16)) + contract_first(
        basis_root, mass_root_x.astype(jnp.bfloat16)
    )
    gram = lax.psum(gram_part, ("leaf", "front"))
    gram_low = gram.astype(jnp.bfloat16)
    new_sub = x_sub - jnp.dot(basis_sub, gram_low, preferred_element_type=jnp.float32)
    new_root = x_root - jnp.dot(basis_root, gram_low, preferred_element_type=jnp.float32)
    return (new_sub, new_root, gram)


def solution(mesh):
    placed = (
        P(("leaf", "front"), None),
        P(("leaf", "front"), None),
        P("leaf", "front", None),
        P("leaf", None, "front"),
        P("leaf", None),
        P(("leaf", "front"), None),
        P(("leaf", "front")),
        P(("leaf", "front")),
        P(("leaf", "front"), None, None),
        P(("leaf", "front"), None),
        P(("leaf", "front"), None),
    )
    return jax.shard_map(
        body,
        mesh=mesh,
        in_specs=placed,
        out_specs=(P(("leaf", "front"), None), P(("leaf", "front"), None), P()),
        check_vma=False,
    )
```

profile of v0, /device:TPU:1, one launch (start us, length us, event | category | flops | bytes accessed | tf_op | source)
XLA Modules:
  0.0 1151.8 jit_solution(42175048578819282)
XLA Ops:
  7.2 1.1 convert_element_type.39
  8.3 16.2 %all_gather.6 = bf16[4096,64]{0,1:T(8,128)(2,1)S(1)} all-gather(bf16[512,64]{0,1:T(8,128)(2,1)S(1)} %convert_element_type.39), channel_id=1, replica_groups=mesh['leaf'=32,'front'=8] {'front'}, dimensions={0}, use_global_device_ids=true | all-gather | bytes 589824 | tf_op jit(solution)/shard_map/all_gather | solution.py:40
  24.5 3.6 fusion.10
  28.2 0.7 convolution_bitcast_fusion
  28.9 1.4 copy.18
  30.3 14.8 %scatter_custom_fusion = f32[12288,64]{1,0:T(8,128)} fusion(s32[2048]{0:T(1024)S(1)} %bitcast.62, f32[2048,64]{1,0:T(8,128)} %copy.18, f32[]{:T(128)} %constant.91.clone.1), kind=kCustom, calls=%fused_computation.4 | custom fusion | flops 131072 | bytes 3146240 | tf_op jit(solution)/shard_map/scatter-add | solution.py:55
  45.1 1.4 subtract_dynamic-update-slice_fusion
  46.5 0.0 all-gather.2.cloned.1.call-start
  46.5 394.9 %reduce-scatter.3.cloned.1.call-done = f32[48,64]{1,0:T(8,128)} async-done(((f32[12288,64]{1,0:T(8,128)}), f32[48,64]{1,0:T(8,128)}) %reduce-scatter.3.cloned.1.call-update) | async-done | bytes 12304 | tf_op jit(solution)/shard_map/reduce_scatter | solution.py:58
  441.4 1.3 negate_convert_fusion
  442.8 0.0 all-reduce.3.cloned.1.call-start
  442.8 112.3 %all-gather.2.cloned.1.call-done = bf16[12288,64]{1,0:T(8,128)(2,1)} async-done(((bf16[48,64]{1,0:T(8,128)(2,1)}), bf16[12288,64]{1,0:T(8,128)(2,1)}) %all-gather.2.cloned.1.call-update) | async-done | bytes 1572880 | tf_op jit(solution)/shard_map/all_gather | solution.py:62
  555.1 4.9 fusion.26
  560.1 262.7 %all-reduce.3.cloned.1.call-done = f32[12288,64]{0,1:T(8,128)} async-done(((f32[12288,64]{0,1:T(8,128)}), f32[12288,64]{0,1:T(8,128)}) %all-reduce.3.cloned.1.call-update) | async-done | bytes 3145744 | tf_op jit(solution)/shard_map/psum | solution.py:66
  822.8 3.2 convert_element_type.43
  826.0 4.1 copy.19
  830.1 7.9 gather_fusion
  838.1 5.1 fusion.8
  843.3 1.1 fusion.47
  844.4 31.3 %reduce-scatter.5.cloned.1.call-done = f32[512,64]{0,1:T(8,128)} async-done(((f32[4096,64]{0,1:T(8,128)}), f32[512,64]{0,1:T(8,128)}) %reduce-scatter.5.cloned.1.call-update) | async-done | bytes 131088 | tf_op jit(solution)/shard_map/reduce_scatter | solution.py:77
  875.6 1.1 fusion.56
  876.7 1.0 collective-permute-start
  877.8 0.1 fusion.24
  877.9 4.1 collective-permute-start.1
  882.0 1.1 collective-permute-done
  883.1 0.2 fusion.23
  883.3 2.9 fusion.4
  886.2 253.0 %all-reduce.5.cloned.1.call-done = f32[2048,64]{0,1:T(8,128)} async-done(((f32[2048,64]{0,1:T(8,128)}), f32[2048,64]{0,1:T(8,128)}) %all-reduce.5.cloned.1.call-update) | async-done | bytes 524304 | tf_op jit(solution)/shard_map/psum | solution.py:93
  1139.3 1.3 fusion.25
  1140.6 0.7 copy.21
  1141.3 3.2 fusion.18
  1144.5 0.8 copy.28
  (36 shorter events, 0.3 us)
Async XLA Ops:
  7.2 21.0 %copy-start = (bf16[1,2048,512]{2,1,0:T(8,128)(2,1)S(1)}, bf16[1,2048,512]{2,1,0:T(8,128)(2,1)}, u32[]{:S(2)}) copy-start(bf16[1,2048,512]{2,1,0:T(8,128)(2,1)} %param.18) | copy-start | bytes 6291460
  7.2 434.2 %reduce-scatter.3.cloned.1.call-start = ((), (), s32[]{:S(2)}) async-start(), calls=%async_computation.2 | async-start | bytes 6316032 | tf_op jit(solution)/shard_map/reduce_scatter | solution.py:58
  28.1 2.1 copy-start.6
  30.3 14.8 %copy-start.7 = (f32[48,64]{1,0:T(8,128)S(1)}, f32[48,64]{1,0:T(8,128)}, u32[]{:S(2)}) copy-start(f32[48,64]{1,0:T(8,128)} %param.16) | copy-start | bytes 36868
  46.5 508.6 %copy-start.1 = (bf16[48,12288]{1,0:T(8,128)(2,1)S(1)}, bf16[48,12288]{1,0:T(8,128)(2,1)}, u32[]{:S(2)}) copy-start(bf16[48,12288]{1,0:T(8,128)(2,1)} %param.20) | copy-start | bytes 3538948
  46.5 508.6 %all-gather.2.cloned.1.call-start = ((), (), s32[]{:S(2)}) async-start(), calls=%async_computation.3 | async-start | bytes 3158016 | tf_op jit(solution)/shard_map/all_gather | solution.py:62
  442.8 380.0 %all-reduce.3.cloned.1.call-start = ((), (), s32[]{:S(2)}) async-start(), calls=%async_computation.4 | async-start | bytes 6291456 | tf_op jit(solution)/shard_map/psum | solution.py:66
  560.0 315.6 %reduce-scatter.5.cloned.1.call-start = ((), (), s32[]{:S(2)}) async-start(), calls=%async_computation.5 | async-start | bytes 1179648 | tf_op jit(solution)/shard_map/reduce_scatter | solution.py:77
  838.0 5.2 copy-start.3
  838.0 5.2 copy-start.9
  838.0 37.6 %copy-start.8 = (f32[512]{0:T(512)S(1)}, f32[512]{0:T(512)}, u32[]{:S(2)}) copy-start(f32[512]{0:T(512)} %param.21) | copy-start | bytes 6148
  838.0 39.7 %copy-start.5 = (bf16[1,256,256]{2,1,0:T(8,128)(2,1)S(1)}, bf16[1,256,256]{2,1,0:T(8,128)(2,1)}, u32[]{:S(2)}) copy-start(bf16[1,256,256]{2,1,0:T(8,128)(2,1)} %param.23) | copy-start | bytes 393220
  843.2 296.1 %all-reduce.5.cloned.1.call-start = ((), (), s32[]{:S(2)}) async-start(), calls=%async_computation.6 | async-start | bytes 1048576 | tf_op jit(solution)/shard_map/psum | solution.py:93
  875.6 265.7 %copy-start.4 = (f32[512,64]{0,1:T(8,128)S(1)}, f32[512,64]{0,1:T(8,128)}, u32[]{:S(2)}) copy-start(f32[512,64]{0,1:T(8,128)} %reduce-scatter.5.cloned.1.call-done) | copy-start | bytes 393220
  876.7 6.4 collective-permute-start
  877.9 5.4 collective-permute-start.1
  1139.3 5.2 copy-start.2
Sparse Core Ops, SparseCore 0:
  46.6 394.7 reduce-scatter.2
  446.3 108.7 all-gather.1
  561.4 261.3 all-reduce.2
  843.3 32.2 reduce-scatter.4
  886.4 252.8 all-reduce.4
where the time goes:
time: 1150 us
  waiting for transfers between devices  1060 us (92%)
  matrix products  23.2 us (2%)
  other arithmetic  22.9 us (2%)
  blocking collectives  16.2 us (1%)
  local copies, waits for them, and re-layouts  14.9 us (1%)
  between operations  14 us (1%)
    reduce_scatter x1, waiting for transfers between devices, body(): lax.psum_scatter(scattered, ('leaf', 'front'), scatter_dimension=0, tiled...  395 us
    psum x1, waiting for transfers between devices, body(): x_full = lax.psum(back_partial, ('leaf', 'front'))  263 us
    psum x1, waiting for transfers between devices, body(): gram = lax.psum(gram_part, ('leaf', 'front'))  253 us
    all_gather x1, waiting for transfers between devices, body(): lax.all_gather(root_mine.astype(jnp.bfloat16), ('leaf', 'front'), axis=0,...  112 us
    reduce_scatter x1, waiting for transfers between devices, body(): lax.psum_scatter(contract_first(columns, t_low), 'front', scatter_dimensi...  31.3 us
  transfers between devices with their start and end apart: 7, of which 6 were waited for; matrix products, arithmetic and copies ran while one was open for 0% of the time, Pallas kernels for 0%

commit v1 on v0

v1 whole, which is shorter than its diff:
```python
import jax
import jax.numpy as jnp
from jax import lax
from jax.experimental import pallas as pl
from jax.experimental.pallas import tpu as pltpu
from jax.sharding import PartitionSpec as P

BF = jnp.bfloat16
F32 = jnp.float32
MESH = pl.DeviceIdType.MESH

N = 64
NF = 8
NY = 4
NZ = 8
SH = 512
SUB = NF * SH
UP = 2048
UPS = UP // NF
RR = 48
GR = NF * RR
SL = NY * GR
ROOT = NF * SL
RIM = 256
NB = 2048
NBS = NB // NF
PAD = 128

STAGES = 25


def dot(a, b):
    return jnp.dot(a, b, preferred_element_type=F32)


def dot_t(a, b):
    return lax.dot_general(a, b, (((1,), (1,)), ((), ())), preferred_element_type=F32)


def kernel(
    rhs_ref,
    rroot_ref,
    factor_hbm,
    coupling_hbm,
    rows_ref,
    froot_hbm,
    mass_ref,
    mroot_ref,
    iface_ref,
    basis_hbm,
    broot_hbm,
    new_sub_ref,
    new_root_ref,
    gram_ref,
    fac,
    cpl,
    onehot,
    frt,
    bas,
    brt,
    rhs_all,
    rr_send,
    rr_all,
    rr_sum,
    y_acc,
    up_send,
    up_recv,
    up_all,
    d_send,
    d_recv,
    d_zsend,
    d_zrecv,
    d_zall,
    d_all,
    yr_all,
    x_send,
    x_recv,
    x_zsend,
    x_zrecv,
    x_zall,
    x_all,
    xr_recv,
    pk_send,
    pk_recv,
    pk_all,
    xs_send,
    xs_recv,
    xs_acc,
    if_send,
    if_recv,
    g_send,
    g_recv,
    g_ysend,
    g_yrecv,
    g_zall,
    g_yall,
    g_all,
    ssem,
    rsem,
    lsem,
):
    g = lax.axis_index("leaf")
    f = lax.axis_index("front")
    z = lax.div(g, NY)
    y = lax.rem(g, NY)

    def dev_f(i):
        return (g, i)

    def dev_y(i):
        return (z * NY + i, f)

    def dev_z(i):
        return (i * NY + y, f)

    nxt = lax.rem(g + 1, NY * NZ)
    prv = lax.rem(g + NY * NZ - 1, NY * NZ)

    barrier = pltpu.get_barrier_semaphore()
    peers = [dev_f(lax.rem(f + k, NF)) for k in range(1, NF)]
    peers += [dev_y(lax.rem(y + k, NY)) for k in range(1, NY)]
    peers += [dev_z(lax.rem(z + k, NZ)) for k in range(1, NZ)]
    peers += [(nxt, f), (prv, f)]
    for dev in peers:
        pl.semaphore_signal(barrier, inc=1, device_id=dev, device_id_type=MESH)

    load_fac = pltpu.make_async_copy(factor_hbm, fac, lsem.at[0])
    load_cpl = pltpu.make_async_copy(coupling_hbm, cpl, lsem.at[1])
    load_bas = pltpu.make_async_copy(basis_hbm, bas, lsem.at[2])
    load_brt = pltpu.make_async_copy(broot_hbm, brt.at[pl.ds(0, RR)], lsem.at[3])
    load_frt = pltpu.make_async_copy(
        froot_hbm.at[:, pl.ds(pl.multiple_of(f * SL, 128), SL)],
        frt.at[pl.ds(pl.multiple_of(f * RR, 16), RR)],
        lsem.at[4],
    )
    load_fac.start()
    load_cpl.start()
    load_frt.start()
    load_bas.start()
    load_brt.start()

    sends = []

    def push(src, dst, stage, k, slot, dev, cond=None):
        copy = pltpu.make_async_remote_copy(
            src_ref=src,
            dst_ref=dst,
            send_sem=ssem.at[stage, k],
            recv_sem=rsem.at[stage, slot],
            device_id=dev,
            device_id_type=MESH,
        )
        if cond is None:
            copy.start()
        else:
            pl.when(cond)(copy.start)
        sends.append((copy, cond))

    def await_slot(buf, stage, slot):
        pltpu.make_async_remote_copy(
            src_ref=buf,
            dst_ref=buf,
            send_sem=ssem.at[stage, 0],
            recv_sem=rsem.at[stage, slot],
            device_id=(g, f),
            device_id_type=MESH,
        ).wait_recv()

    def await_ring(buf, stage, me, n):
        for k in range(1, n):
            p = lax.rem(me + n - k, n)
            await_slot(buf.at[p], stage, p)

    spot = lax.broadcasted_iota(jnp.int32, (PAD, GR), 0)
    lane = lax.broadcasted_iota(jnp.int32, (PAD, GR), 1)
    place = jnp.where((lane == spot + f * RR) & (spot < RR), 1.0, 0.0).astype(BF)
    rr_mine = dot(rroot_ref[...], place).astype(BF)
    rr_send[...] = rr_mine
    rr_all[f] = rr_mine

    pl.semaphore_wait(barrier, len(peers))

    for k in range(1, NF):
        p = lax.rem(f + k, NF)
        push(rhs_ref, rhs_all.at[f], 0, k, f, dev_f(p), f + k < NF)
    push(rr_send, rr_all.at[f], 1, 0, f, dev_f(z), f != z)
    for k in range(1, NF):
        p = lax.rem(f + k, NF)
        push(
            froot_hbm.at[:, pl.ds(pl.multiple_of(p * SL, 128), SL)],
            frt.at[pl.ds(pl.multiple_of(f * RR, 16), RR)],
            2,
            k,
            f,
            dev_f(p),
        )

    def hot(i, _):
        at = pl.multiple_of(i * 64, 64)
        ids = lax.broadcasted_iota(jnp.int32, (64, UP), 0) + (f * SL + i * 64)
        onehot[pl.ds(at, 64), :] = jnp.where(ids == rows_ref[...], 1.0, 0.0).astype(BF)
        return 0

    lax.fori_loop(0, SL // 64, hot, 0)

    load_fac.wait()
    mine = pl.ds(pl.multiple_of(f * SH, 128), SH)
    below = lax.broadcasted_iota(jnp.int32, (SH, SH), 1) <= lax.broadcasted_iota(
        jnp.int32, (SH, SH), 0
    )
    diag = jnp.where(below, fac[:, mine].astype(F32), 0.0).astype(BF)
    fac[:, mine] = diag
    y_acc[...] = dot_t(rhs_ref[...], diag)
    for k in range(1, NF):

        @pl.when(f >= k)
        def _(k=k):
            p = f - k
            await_slot(rhs_all.at[p], 0, p)
            cols = pl.ds(pl.multiple_of(p * SH, 128), SH)
            y_acc[...] += dot_t(rhs_all[p], fac[:, cols])

    y_low = y_acc[...].astype(BF)

    load_cpl.wait()
    for k in range(1, NF + 1):
        p = lax.rem(f + k, NF)
        rows = pl.ds(pl.multiple_of(p * UPS, 128), UPS)
        piece = dot_t(y_low, cpl[rows, :]).astype(BF)
        if k < NF:
            up_send[k] = piece
            push(up_send.at[k], up_recv.at[f], 3, k, f, dev_f(p))
        else:
            up_recv[f] = piece
    await_ring(up_recv, 3, f, NF)
    up_all[f] = sum(up_recv[j].astype(F32) for j in range(NF)).astype(BF)
    for k in range(1, NF):
        push(up_all.at[f], up_all.at[f], 4, k, f, dev_f(lax.rem(f + k, NF)))
    await_ring(up_all, 4, f, NF)

    def leaf_sum(chunk, own, send, recv, zsend, zrecv, zall, full, stage, early=None):
        for k in range(1, NY + 1):
            p = lax.rem(y + k, NY)
            piece = chunk(p)
            if k < NY:
                send[k] = piece.astype(BF)
                push(send.at[k], recv.at[y], stage, k, y, dev_y(p))
            else:
                recv[y] = piece.astype(BF)
        await_ring(recv, stage, y, NY)
        part = sum(recv[j].astype(F32) for j in range(NY))
        part = own(part)
        zsend[...] = part.reshape(NZ, N // NZ, GR)
        zrecv[z] = zsend[z]
        for k in range(1, NZ):
            p = lax.rem(z + k, NZ)
            push(zsend.at[p], zrecv.at[z], stage + 1, k, z, dev_z(p))
        await_ring(zrecv, stage + 1, z, NZ)
        zall[z] = sum(zrecv[j] for j in range(NZ))
        for k in range(1, NZ):
            push(zall.at[z], zall.at[z], stage + 2, k, z, dev_z(lax.rem(z + k, NZ)))
        await_ring(zall, stage + 2, z, NZ)
        full[y] = zall[...].reshape(N, GR).astype(BF)
        for k in range(1, NY):
            push(full.at[y], full.at[y], stage + 3, k, y, dev_y(lax.rem(y + k, NY)))
        if early is not None:
            early()
        await_ring(full, stage + 3, y, NY)
        return jnp.concatenate([full[j] for j in range(NY)], axis=1)

    up_low = jnp.concatenate([up_all[j] for j in range(NF)], axis=1)

    def scatter_chunk(q):
        return -dot_t(up_low, onehot[pl.ds(pl.multiple_of(q * GR, 128), GR), :])

    rr_sum[...] = jnp.zeros_like(rr_sum)

    @pl.when(f == z)
    def _():
        await_ring(rr_all, 1, f, NF)
        rr_sum[...] = sum(rr_all[j].astype(F32) for j in range(NF))

    b_low = leaf_sum(
        scatter_chunk,
        lambda part: part + rr_sum[...],
        d_send,
        d_recv,
        d_zsend,
        d_zrecv,
        d_zall,
        d_all,
        5,
    )

    load_frt.wait()
    for k in range(1, NF):
        p = lax.rem(f + NF - k, NF)
        await_slot(frt.at[pl.ds(pl.multiple_of(p * RR, 16), RR)], 2, p)
    for j in range(NF):
        rows = pl.ds(j * RR, RR)
        row_ids = lax.broadcasted_iota(jnp.int32, (RR, SL), 0) + (g * GR + j * RR)
        col_ids = lax.broadcasted_iota(jnp.int32, (RR, SL), 1) + f * SL
        kept = jnp.where(col_ids <= row_ids, frt[rows, :].astype(F32), 0.0)
        frt[rows, :] = kept.astype(BF)
    yr_all[f] = dot_t(b_low, frt[...]).astype(BF)
    for k in range(1, NF):
        push(yr_all.at[f], yr_all.at[f], 9, k, f, dev_f(lax.rem(f + k, NF)))
    await_ring(yr_all, 9, f, NF)
    yr_low = sum(yr_all[j].astype(F32) for j in range(NF)).astype(BF)

    def back_chunk(q):
        return dot(yr_low, frt[:, pl.ds(pl.multiple_of(q * GR, 128), GR)])

    def hand_block():
        @pl.when(f == z)
        def _():
            xr_recv[...] = x_all[y]

        for k in range(1, NF):
            push(x_all.at[y], xr_recv, 14, k, 0, dev_f(lax.rem(f + k, NF)), f == z)

    x_low = leaf_sum(
        back_chunk,
        lambda part: part,
        x_send,
        x_recv,
        x_zsend,
        x_zrecv,
        x_zall,
        x_all,
        10,
        hand_block,
    )

    for k in range(1, NF + 1):
        p = lax.rem(f + k, NF)
        cols = pl.ds(pl.multiple_of(p * UPS, 128), UPS)
        piece = dot(x_low, onehot[:, cols]).astype(BF)
        if k < NF:
            pk_send[k] = piece
            push(pk_send.at[k], pk_recv.at[f], 15, k, f, dev_f(p))
        else:
            pk_recv[f] = piece
    await_ring(pk_recv, 15, f, NF)
    pk_all[f] = sum(pk_recv[j].astype(F32) for j in range(NF)).astype(BF)
    for k in range(1, NF):
        push(pk_all.at[f], pk_all.at[f], 16, k, f, dev_f(lax.rem(f + k, NF)))
    await_ring(pk_all, 16, f, NF)
    for j in range(NF):
        y_acc[...] -= dot(pk_all[j], cpl[pl.ds(j * UPS, UPS), :])
    t_low = y_acc[...].astype(BF)

    for k in range(1, NF):

        @pl.when(f >= k)
        def _(k=k):
            cols = pl.ds(pl.multiple_of((f - k) * SH, 128), SH)
            xs_send[k] = dot(t_low, fac[:, cols]).astype(BF)

        push(xs_send.at[k], xs_recv.at[f], 17, k, f, dev_f(lax.rem(f + NF - k, NF)), f >= k)
    xs_acc[...] = dot(t_low, fac[:, mine])
    for k in range(1, NF):

        @pl.when(f + k < NF)
        def _(k=k):
            await_slot(xs_recv.at[f + k], 17, f + k)
            xs_acc[...] += xs_recv[f + k].astype(F32)

    xs_low = xs_acc[...].astype(BF)
    if_send[0] = xs_low[:, SH - RIM :]
    push(if_send.at[0], if_recv.at[0], 18, 0, 0, (nxt, f))
    if_send[1] = dot(xs_low[:, :RIM], iface_ref[...]).astype(BF)
    push(if_send.at[1], if_recv.at[1], 19, 0, 0, (prv, f))

    @pl.when(f != z)
    def _():
        await_slot(xr_recv, 14, 0)

    x_own = dot_t(xr_recv[...], place)
    mx_own = (x_own * mroot_ref[...]).astype(BF)

    mass_x = xs_acc[...] * mass_ref[...]
    await_slot(if_recv.at[0], 18, 0)
    first = mass_x[:, :RIM] + dot_t(if_recv[0], iface_ref[...])
    await_slot(if_recv.at[1], 19, 0)
    last = mass_x[:, SH - RIM :] + if_recv[1].astype(F32)
    mx = jnp.concatenate([first, last], axis=1).astype(BF)

    load_bas.wait()
    load_brt.wait()
    brt[pl.ds(RR, PAD - RR), :] = jnp.zeros((PAD - RR, NB), BF)
    for k in range(1, NF + 1):
        p = lax.rem(f + k, NF)
        cols = pl.ds(pl.multiple_of(p * NBS, 128), NBS)
        piece = (dot(mx, bas[:, cols]) + dot(mx_own, brt[:, cols])).astype(BF)
        if k < NF:
            g_send[k] = piece
            push(g_send.at[k], g_recv.at[f], 20, k, f, dev_f(p))
        else:
            g_recv[f] = piece
    await_ring(g_recv, 20, f, NF)
    part = sum(g_recv[j].astype(F32) for j in range(NF)).astype(BF)
    g_ysend[...] = part.reshape(NY, N // NY, NBS)
    g_yrecv[y] = g_ysend[y]
    for k in range(1, NY):
        p = lax.rem(y + k, NY)
        push(g_ysend.at[p], g_yrecv.at[y], 21, k, y, dev_y(p))
    await_ring(g_yrecv, 21, y, NY)
    g_zall[z] = sum(g_yrecv[j].astype(F32) for j in range(NY)).astype(BF)
    for k in range(1, NZ):
        push(g_zall.at[z], g_zall.at[z], 22, k, z, dev_z(lax.rem(z + k, NZ)))
    await_ring(g_zall, 22, z, NZ)
    g_yall[y] = sum(g_zall[j].astype(F32) for j in range(NZ)).astype(BF)
    for k in range(1, NY):
        push(g_yall.at[y], g_yall.at[y], 23, k, y, dev_y(lax.rem(y + k, NY)))
    await_ring(g_yall, 23, y, NY)
    g_all[f] = g_yall[...].reshape(N, NBS)
    for k in range(1, NF):
        push(g_all.at[f], g_all.at[f], 24, k, f, dev_f(lax.rem(f + k, NF)))
    new_sub_ref[...] = xs_acc[...]
    new_root_ref[...] = x_own
    for k in range(NF):
        p = lax.rem(f + NF - k, NF)
        if k:
            await_slot(g_all.at[p], 24, p)
        cols = pl.ds(pl.multiple_of(p * NBS, 128), NBS)
        gram_ref[:, cols] = g_all[p].astype(F32)
        new_sub_ref[...] -= dot_t(g_all[p], bas[:, cols])
        new_root_ref[...] -= dot_t(g_all[p], brt[:, cols])

    for copy, cond in sends:
        if cond is None:
            copy.wait_send()
        else:
            pl.when(cond)(copy.wait_send)


def body(
    rhs_sub,
    rhs_root,
    factor_sub,
    coupling,
    update_rows,
    factor_root,
    mass_sub,
    mass_root,
    interface,
    basis_sub,
    basis_root,
):
    rhs_t = rhs_sub.astype(BF).T
    root_t = jnp.pad(rhs_root.astype(BF).T, ((0, 0), (0, PAD - RR)))
    mroot = jnp.pad(mass_root, (0, PAD - RR))[None, :]
    vmem = pl.BlockSpec(memory_space=pltpu.VMEM)
    hbm = pl.BlockSpec(memory_space=pl.ANY)
    leaf_sum = [
        pltpu.VMEM((NY, N, GR), BF),
        pltpu.VMEM((NY, N, GR), BF),
        pltpu.VMEM((NZ, N // NZ, GR), F32),
        pltpu.VMEM((NZ, N // NZ, GR), F32),
        pltpu.VMEM((NZ, N // NZ, GR), F32),
        pltpu.VMEM((NY, N, GR), BF),
    ]
    new_sub, new_root, gram = pl.pallas_call(
        kernel,
        out_shape=(
            jax.ShapeDtypeStruct((N, SH), F32),
            jax.ShapeDtypeStruct((N, PAD), F32),
            jax.ShapeDtypeStruct((N, NB), F32),
        ),
        in_specs=[vmem, vmem, hbm, hbm, vmem, hbm, vmem, vmem, vmem, hbm, hbm],
        out_specs=(vmem, vmem, vmem),
        scratch_shapes=[
            pltpu.VMEM((SH, SUB), BF),
            pltpu.VMEM((UP, SH), BF),
            pltpu.VMEM((SL, UP), BF),
            pltpu.VMEM((GR, SL), BF),
            pltpu.VMEM((SH, NB), BF),
            pltpu.VMEM((PAD, NB), BF),
            pltpu.VMEM((NF, N, SH), BF),
            pltpu.VMEM((N, GR), BF),
            pltpu.VMEM((NF, N, GR), BF),
            pltpu.VMEM((N, GR), F32),
            pltpu.VMEM((N, SH), F32),
            pltpu.VMEM((NF, N, UPS), BF),
            pltpu.VMEM((NF, N, UPS), BF),
            pltpu.VMEM((NF, N, UPS), BF),
            *leaf_sum,
            pltpu.VMEM((NF, N, GR), BF),
            *leaf_sum,
            pltpu.VMEM((N, GR), BF),
            pltpu.VMEM((NF, N, UPS), BF),
            pltpu.VMEM((NF, N, UPS), BF),
            pltpu.VMEM((NF, N, UPS), BF),
            pltpu.VMEM((NF, N, SH), BF),
            pltpu.VMEM((NF, N, SH), BF),
            pltpu.VMEM((N, SH), F32),
            pltpu.VMEM((2, N, RIM), BF),
            pltpu.VMEM((2, N, RIM), BF),
            pltpu.VMEM((NF, N, NBS), BF),
            pltpu.VMEM((NF, N, NBS), BF),
            pltpu.VMEM((NY, N // NY, NBS), BF),
            pltpu.VMEM((NY, N // NY, NBS), BF),
            pltpu.VMEM((NZ, N // NY, NBS), BF),
            pltpu.VMEM((NY, N // NY, NBS), BF),
            pltpu.VMEM((NF, N, NBS), BF),
            pltpu.SemaphoreType.DMA((STAGES, 8)),
            pltpu.SemaphoreType.DMA((STAGES, 8)),
            pltpu.SemaphoreType.DMA((8,)),
        ],
        compiler_params=pltpu.CompilerParams(
            collective_id=0, has_side_effects=True, vmem_limit_bytes=48 * 1024 * 1024
        ),
    )(
        rhs_t,
        root_t,
        factor_sub[0],
        coupling[0],
        update_rows,
        factor_root,
        mass_sub[None, :],
        mroot,
        interface[0],
        basis_sub,
        basis_root,
    )
    return new_sub.T, new_root[:, :RR].T, gram.T


def solution(mesh):
    placed = (
        P(("leaf", "front"), None),
        P(("leaf", "front"), None),
        P("leaf", "front", None),
        P("leaf", None, "front"),
        P("leaf", None),
        P(("leaf", "front"), None),
        P(("leaf", "front")),
        P(("leaf", "front")),
        P(("leaf", "front"), None, None),
        P(("leaf", "front"), None),
        P(("leaf", "front"), None),
    )
    return jax.shard_map(
        body,
        mesh=mesh,
        in_specs=placed,
        out_specs=(P(("leaf", "front"), None), P(("leaf", "front"), None), P()),
        check_vma=False,
    )
```

time: 1150 us -> 151 us (0.13)
  waiting for transfers between devices: 1060 us -> 0 us
  Pallas kernels: 0 us -> 139 us
  matrix products: 23.2 us -> 0 us
  other arithmetic: 22.9 us -> 1.66 us
  blocking collectives: 16.2 us -> 0 us
  between operations: 14 us -> 0.67 us
    psum x2 -> x0, waiting for transfers between devices: 516 us -> none  [the longest x1 263 us: body(): x_full = lax.psum(back_partial, ('leaf', 'front'))]
    reduce_scatter x2 -> x0, waiting for transfers between devices: 426 us -> none  [the longest x1 395 us: body(): lax.psum_scatter(scattered, ('leaf', 'front'), scatter_dimension=0, tiled...]
    pallas_call x0 -> x1, Pallas kernels: none -> 139 us  [body(): pl.pallas_call(kernel, out_shape=(jax.ShapeDtypeStruct((N, SH), F32), jax...]
    all_gather x1 -> x0, waiting for transfers between devices: 112 us -> none  [body(): lax.all_gather(root_mine.astype(jnp.bfloat16), ('leaf', 'front'), axis=0,...]
    dot_general x10 -> x0, matrix products: 23.2 us -> none  [the longest x5 14.1 us: contract_first(): lax.dot_general(left, right, (((0,), (0,)), ((), ())), preferred_element_...]
    all_gather x1 -> x0, blocking collectives: 16.2 us -> none  [body(): block_rows = lax.all_gather(rhs_low, 'front', axis=0, tiled=True)]
    scatter-add x2 -> x0, other arithmetic: 14.9 us -> none  [the longest x1 14.8 us: body(): jnp.zeros((root_order, width), jnp.float32).at[update_rows[0]]]
  transfers between devices with their start and end apart: 7 -> 0, of which waited for: 6 -> 0; matrix products, arithmetic and copies ran while one was open for 0% -> 0% of each run, Pallas kernels for 0% -> 0%
where the time goes in v1:
time: 151 us; the launch traced here: 150 us
  Pallas kernels  139 us (92%)
  local copies, waits for them, and re-layouts  8.97 us (6%)
  other arithmetic  1.66 us (1%)
    pallas_call x1, Pallas kernels, body(): pl.pallas_call(kernel, out_shape=(jax.ShapeDtypeStruct((N, SH), F32), jax...  139 us
    unnamed x15, local copies, waits for them, and re-layouts  8.2 us

profile of v1, /device:TPU:1, one launch (start us, length us, event | category | flops | bytes accessed | tf_op | source)
XLA Modules:
  0.0 150.3 jit_solution(16907254343741117520)
XLA Ops:
  0.6 0.7 pad_bitcast_fusion.mroot_ref
  1.3 0.7 convert_element_type.11
  2.0 0.1 copy.16
  2.1 0.9 convert_bitcast_fusion.rhs_ref
  3.1 0.0 copy-start
  3.1 1.6 %copy-done = bf16[1,2048,512]{2,1,0:T(8,128)(2,1)S(1)} copy-done((bf16[1,2048,512]{2,1,0:T(8,128)(2,1)S(1)}, bf16[1,2048,512]{2,1,0:T(8,128)(2,1)}, u32[]{:S(2)}) %copy-start) | copy-done | bytes 2097176
  4.7 0.0 copy-start.1
  4.7 1.3 copy-done.1
  5.9 0.0 copy-start.2
  5.9 0.9 copy-done.2
  6.9 0.0 copy-start.3
  6.9 0.9 copy-done.3
  7.8 0.0 copy-start.4
  7.8 0.7 copy-done.4
  8.5 0.0 copy-start.5
  8.5 0.7 copy-done.5
  9.1 139.0 %shard_map.130 = (f32[64,512]{1,0:T(8,128)S(1)}, f32[64,128]{1,0:T(8,128)S(1)}, f32[64,2048]{1,0:T(8,128)S(1)}) custom-call(bf16[64,512]{1,0:T(8,128)(2,1)S(1)} %convert_bitcast_fusion.rhs_ref, bf16[64,128]{1,0:T(8,128)(2,1)S(1)} %pad.8.rroot_ref, bf16[512,4096]{1,0:T(8,128)(2,1)} %bitcast.18, bf16[2048,512]{1,0:T(8,128)(2,1)S(1)} %bitcast.13, ...), custom_call_target="tpu_custom_call" | custom-call | tf_op jit(solution)/shard_map/pallas_call | solution.py:464
  148.2 0.7 copy.17
  148.9 0.7 copy.20
  149.5 0.8 copy.21
  (2 shorter events, 0.0 us)
Async XLA Ops:
  3.1 1.6 %copy-start = (bf16[1,2048,512]{2,1,0:T(8,128)(2,1)S(1)}, bf16[1,2048,512]{2,1,0:T(8,128)(2,1)}, u32[]{:S(2)}) copy-start(bf16[1,2048,512]{2,1,0:T(8,128)(2,1)} %param.14) | copy-start | bytes 6291460
  4.7 1.3 copy-start.1
  5.9 0.9 copy-start.2
  6.9 0.9 copy-start.3
  7.8 0.7 copy-start.4
  8.5 0.7 copy-start.5

commit v2 on v1

v2 whole, which is shorter than its diff:
```python
import jax
import jax.numpy as jnp
from jax import lax
from jax.experimental import pallas as pl
from jax.experimental.pallas import tpu as pltpu
from jax.sharding import PartitionSpec as P

BF = jnp.bfloat16
F32 = jnp.float32
MESH = pl.DeviceIdType.MESH

N = 64
NF = 8
NY = 4
NZ = 8
NX = 4
NC = 2
NG = NY * NZ
NS = 4
NR = NY * NS
SH = 512
SUB = NF * SH
UP = 2048
UPS = UP // NF
RR = 48
GR = NF * RR
SL = NY * GR
ROOT = NF * SL
RIM = 256
NB = 2048
NBS = NB // NF
PAD = 128
SENDS = 240
RECVS = 160


def dot(a, b):
    return jnp.dot(a, b, preferred_element_type=F32)


def dot_t(a, b):
    return lax.dot_general(a, b, (((1,), (1,)), ((), ())), preferred_element_type=F32)


def kernel(
    rhs_hbm,
    rroot_hbm,
    factor_hbm,
    coupling_hbm,
    rows_hbm,
    froot_hbm,
    mass_hbm,
    mroot_hbm,
    iface_hbm,
    basis_hbm,
    broot_hbm,
    new_sub_ref,
    new_root_ref,
    gram_ref,
    rhs_in,
    rroot_in,
    fac,
    cpl,
    rows_ref,
    frs,
    mass_ref,
    mroot_in,
    iface_ref,
    bas,
    brt,
    onehot,
    frt,
    rhs_all,
    rr_send,
    rr_all,
    rr_sum,
    y_acc,
    up_send,
    up_recv,
    up_all,
    d_send,
    d_recv,
    d_all,
    yr_send,
    yr_sib,
    yr_all,
    x_send,
    x_recv,
    x_all,
    xr_recv,
    pk_send,
    pk_recv,
    pk_all,
    xb_send,
    xb_recv,
    xs_send,
    xs_recv,
    xs_acc,
    if_send,
    if_recv,
    gc_send,
    gc_recv,
    gc_own,
    gp_send,
    gp_recv,
    gz_all,
    g_all,
    ssem,
    rsem,
    lsem,
):
    g = lax.axis_index("leaf")
    f = lax.axis_index("front")
    z = lax.div(g, NY)
    y = lax.rem(g, NY)
    x = lax.div(f, NC)
    c = lax.rem(f, NC)
    other = 1 - c

    def dev_f(i):
        return (g, i)

    def dev_x(i):
        return (g, i * NC + c)

    def dev_z(i):
        return (i * NY + y, f)

    def dev_xy(i, j):
        return (z * NY + j, i * NC + c)

    def turn(a, k, n):
        return lax.rem(a + k, n)

    loads = [
        (rhs_hbm, rhs_in),
        (rroot_hbm, rroot_in),
        (rows_hbm, rows_ref),
        (factor_hbm, fac),
        (froot_hbm, frs),
        (coupling_hbm, cpl),
        (iface_hbm, iface_ref),
        (mass_hbm, mass_ref),
        (mroot_hbm, mroot_in),
        (broot_hbm, brt),
        (basis_hbm, bas),
    ]
    loads = [pltpu.make_async_copy(a, b, lsem.at[i]) for i, (a, b) in enumerate(loads)]
    (
        load_rhs,
        load_rroot,
        load_rows,
        load_fac,
        load_frs,
        load_cpl,
        load_iface,
        load_mass,
        load_mroot,
        load_brt,
        load_bas,
    ) = loads
    for load in loads:
        load.start()

    barrier = pltpu.get_barrier_semaphore()
    peers = [dev_f(turn(f, k, NF)) for k in range(1, NF)]
    peers += [(turn(g, k, NG), f) for k in range(1, NG)]
    peers += [
        dev_xy(turn(x, i, NX), turn(y, j, NY)) for i in range(1, NX) for j in range(1, NY)
    ]
    for dev in peers:
        pl.semaphore_signal(barrier, inc=1, device_id=dev, device_id_type=MESH)

    sends = []
    slots = [0]

    def take(n):
        slots[0] += n
        assert slots[0] <= RECVS
        return slots[0] - n

    def push(src, dst, slot, dev, cond=None):
        assert len(sends) < SENDS
        copy = pltpu.make_async_remote_copy(
            src_ref=src,
            dst_ref=dst,
            send_sem=ssem.at[len(sends)],
            recv_sem=rsem.at[slot],
            device_id=dev,
            device_id_type=MESH,
        )
        if cond is None:
            copy.start()
        else:
            pl.when(cond)(copy.start)
        sends.append((copy, cond))

    def land(buf, slot):
        pltpu.make_async_remote_copy(
            src_ref=buf,
            dst_ref=buf,
            send_sem=ssem.at[0],
            recv_sem=rsem.at[slot],
            device_id=(g, f),
            device_id_type=MESH,
        ).wait_recv()

    def land_ring(buf, base, me, n):
        for k in range(1, n):
            p = turn(me, n - k, n)
            land(buf.at[p], base + p)

    spot = lax.broadcasted_iota(jnp.int32, (PAD, GR), 0)
    lane = lax.broadcasted_iota(jnp.int32, (PAD, GR), 1)
    place = jnp.where((lane == spot + f * RR) & (spot < RR), 1.0, 0.0).astype(BF)
    unit = jnp.where(
        lax.broadcasted_iota(jnp.int32, (N, N), 0) == lax.broadcasted_iota(jnp.int32, (N, N), 1),
        1.0,
        0.0,
    ).astype(BF)
    load_rhs.wait()
    rhs_all[f] = rhs_in[...].astype(BF)
    load_rroot.wait()
    rr_mine = dot(dot_t(unit, rroot_in[...].astype(BF)).astype(BF), place[:RR]).astype(BF)
    rr_send[...] = rr_mine
    rr_all[f] = rr_mine

    pl.semaphore_wait(barrier, len(peers))

    at = take(NF)
    for k in range(1, NF):
        push(rhs_all.at[f], rhs_all.at[f], at + f, dev_f(turn(f, k, NF)), f + k < NF)
    at_rhs = at
    at_rr = take(NF)
    push(rr_send, rr_all.at[f], at_rr + f, dev_f(z), f != z)

    load_rows.wait()

    def hot(i, _):
        rows = pl.ds(pl.multiple_of(i * 64, 64), 64)
        ids = lax.broadcasted_iota(jnp.int32, (64, UP), 0) + (f * SL + i * 64)
        onehot[rows, :] = jnp.where(ids == rows_ref[...], 1.0, 0.0).astype(BF)
        return 0

    lax.fori_loop(0, SL // 64, hot, 0)

    load_fac.wait()
    mine = pl.ds(pl.multiple_of(f * SH, 128), SH)
    below = lax.broadcasted_iota(jnp.int32, (SH, SH), 1) <= lax.broadcasted_iota(
        jnp.int32, (SH, SH), 0
    )
    diag = jnp.where(below, fac[:, mine].astype(F32), 0.0).astype(BF)
    fac[:, mine] = diag
    y_acc[...] = dot_t(rhs_all[f], diag)

    load_frs.wait()

    def lower(j, _):
        cols = pl.ds(pl.multiple_of(j * SL, 128), SL)
        row_ids = lax.broadcasted_iota(jnp.int32, (RR, SL), 0) + (g * GR + f * RR)
        col_ids = lax.broadcasted_iota(jnp.int32, (RR, SL), 1) + j * SL
        frs[:, cols] = jnp.where(col_ids <= row_ids, frs[:, cols].astype(F32), 0.0).astype(BF)
        return 0

    lax.fori_loop(0, NF, lower, 0)
    for k in range(1, NF):

        @pl.when(f >= k)
        def _(k=k):
            p = f - k
            land(rhs_all.at[p], at_rhs + p)
            cols = pl.ds(pl.multiple_of(p * SH, 128), SH)
            y_acc[...] += dot_t(rhs_all[p], fac[:, cols])

    y_low = y_acc[...].astype(BF)

    load_cpl.wait()
    at = take(NF)
    for k in range(1, NF + 1):
        p = turn(f, k, NF)
        rows = pl.ds(pl.multiple_of(p * UPS, 128), UPS)
        piece = dot_t(y_low, cpl[rows, :]).astype(BF)
        if k < NF:
            up_send[k] = piece
            push(up_send.at[k], up_recv.at[f], at + f, dev_f(p))
        else:
            up_recv[f] = piece
    land_ring(up_recv, at, f, NF)
    up_all[f] = sum(up_recv[j].astype(F32) for j in range(NF)).astype(BF)
    at = take(NF)
    for k in range(1, NF):
        push(up_all.at[f], up_all.at[f], at + f, dev_f(turn(f, k, NF)))

    at_frt = take(NF)
    my_rows = pl.ds(pl.multiple_of(f * RR, 16), RR)
    for k in range(1, NF):
        p = turn(f, k, NF)
        cols = pl.ds(pl.multiple_of(p * SL, 128), SL)
        push(frs.at[:, cols], frt.at[my_rows], at_frt + f, dev_f(p))
    frt[my_rows, :] = frs[:, pl.ds(pl.multiple_of(f * SL, 128), SL)]

    @pl.when(f == z)
    def _():
        land_ring(rr_all, at_rr, f, NF)
        rr_sum[...] = sum(rr_all[j].astype(F32) for j in range(NF))

    @pl.when(f != z)
    def _():
        rr_sum[...] = jnp.zeros_like(rr_sum)

    land_ring(up_all, at, f, NF)

    adds = lax.rem(z + y + c, 2) == 0
    spot_mine = 2 * z + lax.div(y, 2)

    def leaf_sum(chunk, send, recv, full):
        at_sum = take(1)
        at_full = take(1)
        for turn_q in (2, 1, 3, 0):
            q = turn(lax.div(z, 2), turn_q, NY)
            send[q] = chunk(q).astype(BF).reshape(NS, N // NS, GR)
            for s in range(NS):
                zi = 2 * q + s // 2
                to = zi * NY + 2 * (s % 2) + lax.rem(zi + c, 2)
                slot = lax.rem(g - to + NG - 1, NG)
                push(send.at[q, s], recv.at[slot], at_sum, (to, f), to != g)

        @pl.when(adds)
        def _():
            land(recv.at[pl.ds(0, NG - 1)], at_sum)
            q = lax.div(spot_mine, NS)
            total = send[q, lax.rem(spot_mine, NS)].astype(F32)
            for j in range(NG - 1):
                total += recv[j].astype(F32)
            full[spot_mine] = total.astype(BF)

        for k in sorted(range(1, NG), key=lambda k: -min(k, NG - k)):
            to = turn(g, k, NG)
            push(full.at[spot_mine], full.at[spot_mine], at_full, (to, f), adds)

        @pl.when(adds)
        def _():
            land(full.at[pl.ds(0, NR - 1)], at_full)

        @pl.when(jnp.logical_not(adds))
        def _():
            land(full, at_full)

        parts = [full[pl.ds(NS * j, NS)].reshape(N, GR) for j in range(NY)]
        return jnp.concatenate(parts, axis=1)

    up_low = jnp.concatenate([up_all[j] for j in range(NF)], axis=1)

    def scatter_chunk(q):
        total = dot_t(up_low, onehot[pl.ds(pl.multiple_of(q * GR, 128), GR), :])
        return jnp.where(q == y, rr_sum[...], 0.0) - total

    b_low = leaf_sum(scatter_chunk, d_send, d_recv, d_all)

    land_ring_rows = [turn(f, NF - k, NF) for k in range(1, NF)]
    for p in land_ring_rows:
        land(frt.at[pl.ds(pl.multiple_of(p * RR, 16), RR)], at_frt + p)
    yr_send[...] = dot_t(b_low, frt[...]).astype(BF)
    at = take(1)
    push(yr_send, yr_sib, at, dev_f(x * NC + other))
    land(yr_sib, at)
    yr_all[x] = (yr_send[...].astype(F32) + yr_sib[...].astype(F32)).astype(BF)
    at = take(NX)
    for k in (2, 1, 3):
        push(yr_all.at[x], yr_all.at[x], at + x, dev_x(turn(x, k, NX)))
    land_ring(yr_all, at, x, NX)
    yr_low = sum(yr_all[j].astype(F32) for j in range(NX)).astype(BF)

    def back_chunk(q):
        return dot(yr_low, frt[:, pl.ds(pl.multiple_of(q * GR, 128), GR)])

    x_low = leaf_sum(back_chunk, x_send, x_recv, x_all)

    at = take(NF)
    for k in range(1, NF + 1):
        p = turn(f, k, NF)
        cols = pl.ds(pl.multiple_of(p * UPS, 128), UPS)
        piece = dot(x_low, onehot[:, cols]).astype(BF)
        if k < NF:
            pk_send[k] = piece
            push(pk_send.at[k], pk_recv.at[f], at + f, dev_f(p))
        else:
            pk_recv[f] = piece
    land_ring(pk_recv, at, f, NF)
    pk_all[f] = sum(pk_recv[j].astype(F32) for j in range(NF)).astype(BF)
    at = take(NF)
    for k in range(1, NF):
        push(pk_all.at[f], pk_all.at[f], at + f, dev_f(turn(f, k, NF)))
    at_xr = take(1)
    block = pl.ds(pl.multiple_of(NS * y, NS), NS)
    for k in range(1, NF):
        push(x_all.at[block], xr_recv, at_xr, dev_f(turn(f, k, NF)), f == z)

    @pl.when(f == z)
    def _():
        xr_recv[...] = x_all[block]

    for k in range(NF):
        p = turn(f, NF - k, NF)
        if k:
            land(pk_all.at[p], at + p)
        rows = pl.ds(pl.multiple_of(p * UPS, 128), UPS)
        y_acc[...] -= dot(pk_all[p], cpl[rows, :])
    t_low = y_acc[...].astype(BF)

    at = take(NX)
    for k in range(NX):
        used = (x >= k) if k else (c == 1)
        i = turn(x, NX - k, NX)

        @pl.when(used)
        def _(i=i):
            cols = pl.ds(pl.multiple_of((i * NC + other) * SH, 128), SH)
            xb_send[i] = dot(t_low, fac[:, cols]).astype(BF)

        push(xb_send.at[i], xb_recv.at[i], at + i, dev_f(x * NC + other), used)
    at_xs = take(NX)
    for k in (1, 2, 3, 0):
        used = x >= k
        i = turn(x, NX - k, NX)
        cols = pl.ds(pl.multiple_of((i * NC + c) * SH, 128), SH)
        if k:

            @pl.when(used)
            def _(i=i, cols=cols):
                part = dot(t_low, fac[:, cols])
                land(xb_recv.at[i], at + i)
                xs_send[i] = (part + xb_recv[i].astype(F32)).astype(BF)

            push(xs_send.at[i], xs_recv.at[x], at_xs + x, dev_x(i), used)
        else:
            xs_acc[...] = dot(t_low, fac[:, cols])

            @pl.when(c == 0)
            def _(i=i):
                land(xb_recv.at[i], at + i)
                xs_acc[...] += xb_recv[i].astype(F32)

    for k in range(1, NX):

        @pl.when(x + k < NX)
        def _(k=k):
            land(xs_recv.at[x + k], at_xs + x + k)
            xs_acc[...] += xs_recv[x + k].astype(F32)

    at_next = take(1)
    at_prev = take(1)
    xs_low = xs_acc[...].astype(BF)
    if_send[0] = xs_low[:, SH - RIM :]
    push(if_send.at[0], if_recv.at[0], at_next, (turn(g, 1, NG), f))
    load_iface.wait()
    if_send[1] = dot(xs_low[:, :RIM], iface_ref[...]).astype(BF)
    push(if_send.at[1], if_recv.at[1], at_prev, (turn(g, NG - 1, NG), f))

    @pl.when(f != z)
    def _():
        land(xr_recv, at_xr)

    load_mroot.wait()
    x_own = dot_t(xr_recv[...].reshape(N, GR), place)
    new_root_ref[...] = dot_t(place, xr_recv[...].reshape(N, GR))[:RR]
    mx_own = (x_own[:, :RR] * mroot_in[...]).astype(BF)
    load_brt.wait()

    load_mass.wait()
    mass_x = xs_acc[...] * mass_ref[...]
    new_sub_ref[...] = xs_acc[...]
    land(if_recv.at[0], at_next)
    first = mass_x[:, :RIM] + dot_t(if_recv[0], iface_ref[...])
    land(if_recv.at[1], at_prev)
    last = mass_x[:, SH - RIM :] + if_recv[1].astype(F32)
    mx = jnp.concatenate([first, last], axis=1).astype(BF)

    load_bas.wait()

    def gram_part(block):
        cols = pl.ds(pl.multiple_of(block * NBS, 128), NBS)
        return dot(mx, bas[:, cols]) + dot(mx_own, brt[:, cols])

    at = take(NX)
    for j in range(NX):
        gc_send[j] = gram_part(other * NX + j).astype(BF)
        push(gc_send.at[j], gc_recv.at[j], at + j, dev_f(x * NC + other))
    for j in range(NX):
        gc_own[j] = gram_part(c * NX + j)
    at_p = take(1)
    for i in (2, 1, 3, 0):
        xi = turn(x, i, NX)
        land(gc_recv.at[xi], at + xi)
        part = gc_own[xi] + gc_recv[xi].astype(F32)
        gp_send[xi] = part.astype(BF).reshape(NY, N // NY, NBS)
        for j in (2, 1, 3, 0):
            if i or j:
                yj = turn(y, j, NY)
                slot = ((NX - i) % NX) * NY + (NY - j) % NY - 1
                push(gp_send.at[xi, yj], gp_recv.at[slot], at_p, dev_xy(xi, yj))
    land(gp_recv, at_p)
    total = gp_send[x, y].astype(F32)
    for j in range(NX * NY - 1):
        total += gp_recv[j].astype(F32)
    gz_all[z] = total.astype(BF)
    at = take(NZ)
    for k in (4, 3, 5, 2, 6, 1, 7):
        push(gz_all.at[z], gz_all.at[z], at + z, dev_z(turn(z, k, NZ)))
    land_ring(gz_all, at, z, NZ)
    mine = c * NX + x
    g_all[mine, y] = sum(gz_all[j].astype(F32) for j in range(NZ)).astype(BF)
    at = take(1)
    for i in (2, 1, 3, 0):
        for j in (2, 1, 3, 0):
            if i or j:
                to = dev_xy(turn(x, i, NX), turn(y, j, NY))
                push(g_all.at[mine, y], g_all.at[mine, y], at, to)
    land(gp_recv, at)
    at = take(1)
    half = pl.ds(pl.multiple_of(c * NX, NX), NX)
    push(g_all.at[half], g_all.at[half], at, dev_f(x * NC + other))

    def apply(block):
        cols = pl.ds(pl.multiple_of(block * NBS, 128), NBS)
        low = g_all[block].reshape(N, NBS)
        gram_ref[:, cols] = low.astype(F32)
        new_sub_ref[...] -= dot_t(low, bas[:, cols])
        new_root_ref[...] -= dot_t(brt[:, cols], low)

    for j in range(NX):
        apply(c * NX + j)
    land(g_all.at[pl.ds(pl.multiple_of(other * NX, NX), NX)], at)
    for j in range(NX):
        apply(other * NX + j)

    for copy, cond in sends:
        if cond is None:
            copy.wait_send()
        else:
            pl.when(cond)(copy.wait_send)


def body(
    rhs_sub,
    rhs_root,
    factor_sub,
    coupling,
    update_rows,
    factor_root,
    mass_sub,
    mass_root,
    interface,
    basis_sub,
    basis_root,
):
    vmem = pl.BlockSpec(memory_space=pltpu.VMEM)
    hbm = pl.BlockSpec(memory_space=pl.ANY)
    leaf_sum = [
        pltpu.VMEM((NY, NS, N // NS, GR), BF),
        pltpu.VMEM((NG, N // NS, GR), BF),
        pltpu.VMEM((NR, N // NS, GR), BF),
    ]
    new_sub, new_root, gram = pl.pallas_call(
        kernel,
        out_shape=(
            jax.ShapeDtypeStruct((N, SH), F32),
            jax.ShapeDtypeStruct((RR, N), F32),
            jax.ShapeDtypeStruct((N, NB), F32),
        ),
        in_specs=[hbm] * 11,
        out_specs=(vmem, vmem, vmem),
        scratch_shapes=[
            pltpu.VMEM((N, SH), F32),
            pltpu.VMEM((RR, N), F32),
            pltpu.VMEM((SH, SUB), BF),
            pltpu.VMEM((UP, SH), BF),
            pltpu.VMEM((1, UP), jnp.int32),
            pltpu.VMEM((RR, ROOT), BF),
            pltpu.VMEM((1, SH), F32),
            pltpu.VMEM((1, RR), F32),
            pltpu.VMEM((RIM, RIM), BF),
            pltpu.VMEM((SH, NB), BF),
            pltpu.VMEM((RR, NB), BF),
            pltpu.VMEM((SL, UP), BF),
            pltpu.VMEM((GR, SL), BF),
            pltpu.VMEM((NF, N, SH), BF),
            pltpu.VMEM((N, GR), BF),
            pltpu.VMEM((NF, N, GR), BF),
            pltpu.VMEM((N, GR), F32),
            pltpu.VMEM((N, SH), F32),
            pltpu.VMEM((NF, N, UPS), BF),
            pltpu.VMEM((NF, N, UPS), BF),
            pltpu.VMEM((NF, N, UPS), BF),
            *leaf_sum,
            pltpu.VMEM((N, GR), BF),
            pltpu.VMEM((N, GR), BF),
            pltpu.VMEM((NX, N, GR), BF),
            *leaf_sum,
            pltpu.VMEM((NS, N // NS, GR), BF),
            pltpu.VMEM((NF, N, UPS), BF),
            pltpu.VMEM((NF, N, UPS), BF),
            pltpu.VMEM((NF, N, UPS), BF),
            pltpu.VMEM((NX, N, SH), BF),
            pltpu.VMEM((NX, N, SH), BF),
            pltpu.VMEM((NX, N, SH), BF),
            pltpu.VMEM((NX, N, SH), BF),
            pltpu.VMEM((N, SH), F32),
            pltpu.VMEM((2, N, RIM), BF),
            pltpu.VMEM((2, N, RIM), BF),
            pltpu.VMEM((NX, N, NBS), BF),
            pltpu.VMEM((NX, N, NBS), BF),
            pltpu.VMEM((NX, N, NBS), F32),
            pltpu.VMEM((NX, NY, N // NY, NBS), BF),
            pltpu.VMEM((NX * NY - 1, N // NY, NBS), BF),
            pltpu.VMEM((NZ, N // NY, NBS), BF),
            pltpu.VMEM((NF, NY, N // NY, NBS), BF),
            pltpu.SemaphoreType.DMA((SENDS,)),
            pltpu.SemaphoreType.DMA((RECVS,)),
            pltpu.SemaphoreType.DMA((16,)),
        ],
        compiler_params=pltpu.CompilerParams(
            collective_id=0, has_side_effects=True, vmem_limit_bytes=56 * 1024 * 1024
        ),
    )(
        rhs_sub.T,
        rhs_root,
        factor_sub[0],
        coupling[0],
        update_rows,
        factor_root,
        mass_sub[None, :],
        mass_root[None, :],
        interface[0],
        basis_sub,
        basis_root,
    )
    return new_sub.T, new_root, gram.T


def solution(mesh):
    placed = (
        P(("leaf", "front"), None),
        P(("leaf", "front"), None),
        P("leaf", "front", None),
        P("leaf", None, "front"),
        P("leaf", None),
        P(("leaf", "front"), None),
        P(("leaf", "front")),
        P(("leaf", "front")),
        P(("leaf", "front"), None, None),
        P(("leaf", "front"), None),
        P(("leaf", "front"), None),
    )
    return jax.shard_map(
        body,
        mesh=mesh,
        in_specs=placed,
        out_specs=(P(("leaf", "front"), None), P(("leaf", "front"), None), P()),
        check_vma=False,
    )
```

time: 151 us -> 120 us (0.79)
  Pallas kernels: 139 us -> 114 us
  local copies, waits for them, and re-layouts: 8.97 us -> 4.79 us
  other arithmetic: 1.66 us -> 0 us
    pallas_call x1, Pallas kernels: 139 us -> 114 us  [body(): pl.pallas_call(kernel, out_shape=(jax.ShapeDtypeStruct((N, SH), F32), jax...]
    unnamed x15 -> x3, local copies, waits for them, and re-layouts: 8.2 us -> 4.79 us
where the time goes in v2:
time: 120 us; the launch traced here: 119 us
  Pallas kernels  114 us (95%)
  local copies, waits for them, and re-layouts  4.79 us (4%)
    pallas_call x1, Pallas kernels, body(): pl.pallas_call(kernel, out_shape=(jax.ShapeDtypeStruct((N, SH), F32), jax...  114 us
    unnamed x3, local copies, waits for them, and re-layouts  4.79 us

profile of v2, /device:TPU:1, one launch (start us, length us, event | category | flops | bytes accessed | tf_op | source)
XLA Modules:
  0.0 119.4 jit_solution(9930449767148813454)
XLA Ops:
  0.6 114.0 %shard_map.130 = (f32[64,512]{1,0:T(8,128)}, f32[48,64]{1,0:T(8,128)}, f32[64,2048]{1,0:T(8,128)}) custom-call(f32[64,512]{1,0:T(8,128)} %bitcast.11, f32[48,64]{1,0:T(8,128)} %rroot_hbm.1, bf16[512,4096]{1,0:T(8,128)(2,1)} %bitcast.8, bf16[2048,512]{1,0:T(8,128)(2,1)} %bitcast.9, s32[1,2048]{1,0:T(1,128)} %rows_hbm.1, bf16[48,12288]{1,0:T(8,128)(2,1)} %froot_hbm.1, ...), custom_call_target="tpu_custom_call" | custom-call | tf_op jit(solution)/shard_map/pallas_call | solution.py:564
  114.6 1.6 %copy.17 = f32[512,64]{0,1:T(8,128)} copy(f32[512,64]{0,1:T(8,128)} %bitcast.13) | data formatting | bytes 262144
  116.2 1.3 %copy.18 = f32[48,64]{1,0:T(8,128)} copy(f32[48,64]{1,0:T(8,128)} %get-tuple-element.13) | data formatting | bytes 24576
  117.6 1.9 %copy.19 = f32[2048,64]{0,1:T(8,128)} copy(f32[2048,64]{0,1:T(8,128)} %bitcast.10) | data formatting | bytes 1048576

commit v3 on v2

--- a/solution.py
+++ b/solution.py
@@ -30,6 +30,8 @@
 NB = 2048
 NBS = NB // NF
 PAD = 128
+STEP = 4
+ORDER = (4, 5, 3, 2, 6, 7, 1)
 SENDS = 240
 RECVS = 160
 
@@ -54,9 +56,9 @@
     iface_hbm,
     basis_hbm,
     broot_hbm,
-    new_sub_ref,
-    new_root_ref,
-    gram_ref,
+    xs_hbm,
+    xr_hbm,
+    g_hbm,
     rhs_in,
     rroot_in,
     fac,
@@ -87,6 +89,7 @@
     x_send,
     x_recv,
     x_all,
+    xr_send,
     xr_recv,
     pk_send,
     pk_recv,
@@ -96,6 +99,7 @@
     xs_send,
     xs_recv,
     xs_acc,
+    xr_out,
     if_send,
     if_recv,
     gc_send,
@@ -163,12 +167,23 @@
         load.start()
 
     barrier = pltpu.get_barrier_semaphore()
-    peers = [dev_f(turn(f, k, NF)) for k in range(1, NF)]
-    peers += [(turn(g, k, NG), f) for k in range(1, NG)]
+    def hops(k, n):
+        return min(k, n - k)
+
+    peers = [(hops(i, NX), (g, turn(x, i, NX) * NC + c)) for i in range(1, NX)]
+    peers += [(hops(i, NX), (g, turn(x, i, NX) * NC + other)) for i in range(NX)]
     peers += [
-        dev_xy(turn(x, i, NX), turn(y, j, NY)) for i in range(1, NX) for j in range(1, NY)
+        (hops(j, NY) + hops(i, NZ), (turn(z, i, NZ) * NY + turn(y, j, NY), f))
+        for i in range(NZ)
+        for j in range(NY)
+        if i or j
     ]
-    for dev in peers:
+    peers += [
+        (hops(i, NX) + hops(j, NY), dev_xy(turn(x, i, NX), turn(y, j, NY)))
+        for i in range(1, NX)
+        for j in range(1, NY)
+    ]
+    for _, dev in sorted(peers, key=lambda peer: -peer[0]):
         pl.semaphore_signal(barrier, inc=1, device_id=dev, device_id_type=MESH)
 
     sends = []
@@ -212,7 +227,16 @@
 
     spot = lax.broadcasted_iota(jnp.int32, (PAD, GR), 0)
     lane = lax.broadcasted_iota(jnp.int32, (PAD, GR), 1)
-    place = jnp.where((lane == spot + f * RR) & (spot < RR), 1.0, 0.0).astype(BF)
+
+    def place(j):
+        return jnp.where((lane == spot + j * RR) & (spot < RR), 1.0, 0.0).astype(BF)
+
+    widen = jnp.where(
+        lax.broadcasted_iota(jnp.int32, (RR, PAD), 0)
+        == lax.broadcasted_iota(jnp.int32, (RR, PAD), 1),
+        1.0,
+        0.0,
+    ).astype(BF)
     unit = jnp.where(
         lax.broadcasted_iota(jnp.int32, (N, N), 0) == lax.broadcasted_iota(jnp.int32, (N, N), 1),
         1.0,
@@ -221,7 +245,7 @@
     load_rhs.wait()
     rhs_all[f] = rhs_in[...].astype(BF)
     load_rroot.wait()
-    rr_mine = dot(dot_t(unit, rroot_in[...].astype(BF)).astype(BF), place[:RR]).astype(BF)
+    rr_mine = dot(dot_t(unit, rroot_in[...].astype(BF)).astype(BF), widen).astype(BF)
     rr_send[...] = rr_mine
     rr_all[f] = rr_mine
 
@@ -276,20 +300,32 @@
 
     load_cpl.wait()
     at = take(NF)
-    for k in range(1, NF + 1):
+    for k in ORDER + (0,):
         p = turn(f, k, NF)
         rows = pl.ds(pl.multiple_of(p * UPS, 128), UPS)
         piece = dot_t(y_low, cpl[rows, :]).astype(BF)
-        if k < NF:
+        if k:
             up_send[k] = piece
             push(up_send.at[k], up_recv.at[f], at + f, dev_f(p))
         else:
             up_recv[f] = piece
+
+    @pl.when(f == z)
+    def _():
+        land_ring(rr_all, at_rr, f, NF)
+        rr_sum[...] = sum(dot(rr_all[j], place(j)) for j in range(NF))
+
+    @pl.when(f != z)
+    def _():
+        rr_sum[...] = jnp.zeros_like(rr_sum)
+
     land_ring(up_recv, at, f, NF)
     up_all[f] = sum(up_recv[j].astype(F32) for j in range(NF)).astype(BF)
     at = take(NF)
-    for k in range(1, NF):
+    for k in ORDER:
         push(up_all.at[f], up_all.at[f], at + f, dev_f(turn(f, k, NF)))
+
+    land_ring(up_all, at, f, NF)
 
     at_frt = take(NF)
     my_rows = pl.ds(pl.multiple_of(f * RR, 16), RR)
@@ -298,17 +334,6 @@
         cols = pl.ds(pl.multiple_of(p * SL, 128), SL)
         push(frs.at[:, cols], frt.at[my_rows], at_frt + f, dev_f(p))
     frt[my_rows, :] = frs[:, pl.ds(pl.multiple_of(f * SL, 128), SL)]
-
-    @pl.when(f == z)
-    def _():
-        land_ring(rr_all, at_rr, f, NF)
-        rr_sum[...] = sum(rr_all[j].astype(F32) for j in range(NF))
-
-    @pl.when(f != z)
-    def _():
-        rr_sum[...] = jnp.zeros_like(rr_sum)
-
-    land_ring(up_all, at, f, NF)
 
     adds = lax.rem(z + y + c, 2) == 0
     spot_mine = 2 * z + lax.div(y, 2)
@@ -377,30 +402,33 @@
     x_low = leaf_sum(back_chunk, x_send, x_recv, x_all)
 
     at = take(NF)
-    for k in range(1, NF + 1):
+    for k in ORDER + (0,):
         p = turn(f, k, NF)
         cols = pl.ds(pl.multiple_of(p * UPS, 128), UPS)
         piece = dot(x_low, onehot[:, cols]).astype(BF)
-        if k < NF:
+        if k:
             pk_send[k] = piece
             push(pk_send.at[k], pk_recv.at[f], at + f, dev_f(p))
         else:
             pk_recv[f] = piece
+    at_xr = take(1)
+
+    @pl.when(f == z)
+    def _():
+        block = x_all[pl.ds(pl.multiple_of(NS * y, NS), NS)].reshape(N, GR)
+        for j in range(NF):
+            xr_send[j] = dot_t(block, place(j)).astype(BF)
+        xr_recv[...] = xr_send[f]
+
+    for k in ORDER:
+        p = turn(f, k, NF)
+        push(xr_send.at[p], xr_recv, at_xr, dev_f(p), f == z)
     land_ring(pk_recv, at, f, NF)
     pk_all[f] = sum(pk_recv[j].astype(F32) for j in range(NF)).astype(BF)
     at = take(NF)
-    for k in range(1, NF):
+    for k in ORDER:
         push(pk_all.at[f], pk_all.at[f], at + f, dev_f(turn(f, k, NF)))
-    at_xr = take(1)
-    block = pl.ds(pl.multiple_of(NS * y, NS), NS)
-    for k in range(1, NF):
-        push(x_all.at[block], xr_recv, at_xr, dev_f(turn(f, k, NF)), f == z)
-
-    @pl.when(f == z)
-    def _():
-        xr_recv[...] = x_all[block]
-
-    for k in range(NF):
+    for k in (0,) + ORDER[::-1]:
         p = turn(f, NF - k, NF)
         if k:
             land(pk_all.at[p], at + p)
@@ -451,6 +479,8 @@
     at_next = take(1)
     at_prev = take(1)
     xs_low = xs_acc[...].astype(BF)
+    keep_sub = pltpu.make_async_copy(xs_acc, xs_hbm, lsem.at[11])
+    keep_sub.start()
     if_send[0] = xs_low[:, SH - RIM :]
     push(if_send.at[0], if_recv.at[0], at_next, (turn(g, 1, NG), f))
     load_iface.wait()
@@ -462,14 +492,14 @@
         land(xr_recv, at_xr)
 
     load_mroot.wait()
-    x_own = dot_t(xr_recv[...].reshape(N, GR), place)
-    new_root_ref[...] = dot_t(place, xr_recv[...].reshape(N, GR))[:RR]
-    mx_own = (x_own[:, :RR] * mroot_in[...]).astype(BF)
+    xr_out[...] = dot_t(widen, xr_recv[...])
+    keep_root = pltpu.make_async_copy(xr_out, xr_hbm, lsem.at[12])
+    keep_root.start()
+    mx_own = (xr_recv[...].astype(F32)[:, :RR] * mroot_in[...]).astype(BF)
     load_brt.wait()
 
     load_mass.wait()
     mass_x = xs_acc[...] * mass_ref[...]
-    new_sub_ref[...] = xs_acc[...]
     land(if_recv.at[0], at_next)
     first = mass_x[:, :RIM] + dot_t(if_recv[0], iface_ref[...])
     land(if_recv.at[1], at_prev)
@@ -521,24 +551,34 @@
     half = pl.ds(pl.multiple_of(c * NX, NX), NX)
     push(g_all.at[half], g_all.at[half], at, dev_f(x * NC + other))
 
-    def apply(block):
-        cols = pl.ds(pl.multiple_of(block * NBS, 128), NBS)
-        low = g_all[block].reshape(N, NBS)
-        gram_ref[:, cols] = low.astype(F32)
-        new_sub_ref[...] -= dot_t(low, bas[:, cols])
-        new_root_ref[...] -= dot_t(brt[:, cols], low)
-
-    for j in range(NX):
-        apply(c * NX + j)
-    land(g_all.at[pl.ds(pl.multiple_of(other * NX, NX), NX)], at)
-    for j in range(NX):
-        apply(other * NX + j)
+    keep_mine = pltpu.make_async_copy(g_all.at[half], g_hbm.at[half], lsem.at[13])
+    keep_mine.start()
+    rest = pl.ds(pl.multiple_of(other * NX, NX), NX)
+    land(g_all.at[rest], at)
+    keep_rest = pltpu.make_async_copy(g_all.at[rest], g_hbm.at[rest], lsem.at[14])
+    keep_rest.start()
 
     for copy, cond in sends:
         if cond is None:
             copy.wait_send()
         else:
             pl.when(cond)(copy.wait_send)
+    for keep in (keep_sub, keep_root, keep_mine, keep_rest):
+        keep.wait()
+
+
+def finish(xs_ref, xr_ref, g_ref, bas_ref, brt_ref, new_sub_ref, new_root_ref, gram_ref):
+    @pl.when(pl.program_id(0) == 0)
+    def _():
+        new_sub_ref[...] = xs_ref[...]
+        new_root_ref[...] = xr_ref[...]
+
+    for j in range(STEP):
+        cols = pl.ds(j * NBS, NBS)
+        low = g_ref[j].reshape(N, NBS)
+        gram_ref[:, cols] = low.astype(F32)
+        new_sub_ref[...] -= dot_t(low, bas_ref[:, cols])
+        new_root_ref[...] -= dot_t(brt_ref[:, cols], low)
 
 
 def body(
@@ -554,22 +594,21 @@
     basis_sub,
     basis_root,
 ):
-    vmem = pl.BlockSpec(memory_space=pltpu.VMEM)
     hbm = pl.BlockSpec(memory_space=pl.ANY)
     leaf_sum = [
         pltpu.VMEM((NY, NS, N // NS, GR), BF),
         pltpu.VMEM((NG, N // NS, GR), BF),
         pltpu.VMEM((NR, N // NS, GR), BF),
     ]
-    new_sub, new_root, gram = pl.pallas_call(
+    xs, xr, low = pl.pallas_call(
         kernel,
         out_shape=(
             jax.ShapeDtypeStruct((N, SH), F32),
             jax.ShapeDtypeStruct((RR, N), F32),
-            jax.ShapeDtypeStruct((N, NB), F32),
+            jax.ShapeDtypeStruct((NF, NY, N // NY, NBS), BF),
         ),
         in_specs=[hbm] * 11,
-        out_specs=(vmem, vmem, vmem),
+        out_specs=(hbm, hbm, hbm),
         scratch_shapes=[
             pltpu.VMEM((N, SH), F32),
             pltpu.VMEM((RR, N), F32),
@@ -585,8 +624,8 @@
             pltpu.VMEM((SL, UP), BF),
             pltpu.VMEM((GR, SL), BF),
             pltpu.VMEM((NF, N, SH), BF),
-            pltpu.VMEM((N, GR), BF),
-            pltpu.VMEM((NF, N, GR), BF),
+            pltpu.VMEM((N, PAD), BF),
+            pltpu.VMEM((NF, N, PAD), BF),
             pltpu.VMEM((N, GR), F32),
             pltpu.VMEM((N, SH), F32),
             pltpu.VMEM((NF, N, UPS), BF),
@@ -597,7 +636,8 @@
             pltpu.VMEM((N, GR), BF),
             pltpu.VMEM((NX, N, GR), BF),
             *leaf_sum,
-            pltpu.VMEM((NS, N // NS, GR), BF),
+            pltpu.VMEM((NF, N, PAD), BF),
+            pltpu.VMEM((N, PAD), BF),
             pltpu.VMEM((NF, N, UPS), BF),
             pltpu.VMEM((NF, N, UPS), BF),
             pltpu.VMEM((NF, N, UPS), BF),
@@ -606,6 +646,7 @@
             pltpu.VMEM((NX, N, SH), BF),
             pltpu.VMEM((NX, N, SH), BF),
             pltpu.VMEM((N, SH), F32),
+            pltpu.VMEM((RR, N), F32),
             pltpu.VMEM((2, N, RIM), BF),
             pltpu.VMEM((2, N, RIM), BF),
             pltpu.VMEM((NX, N, NBS), BF),
@@ -635,6 +676,25 @@
         basis_sub,
         basis_root,
     )
+    whole = pl.BlockSpec((N, SH), lambda i: (0, 0))
+    root = pl.BlockSpec((RR, N), lambda i: (0, 0))
+    new_sub, new_root, gram = pl.pallas_call(
+        finish,
+        grid=(NF // STEP,),
+        out_shape=(
+            jax.ShapeDtypeStruct((N, SH), F32),
+            jax.ShapeDtypeStruct((RR, N), F32),
+            jax.ShapeDtypeStruct((N, NB), F32),
+        ),
+        in_specs=[
+            whole,
+            root,
+            pl.BlockSpec((STEP, NY, N // NY, NBS), lambda i: (i, 0, 0, 0)),
+            pl.BlockSpec((SH, STEP * NBS), lambda i: (0, i)),
+            pl.BlockSpec((RR, STEP * NBS), lambda i: (0, i)),
+        ],
+        out_specs=(whole, root, pl.BlockSpec((N, STEP * NBS), lambda i: (0, i))),
+    )(xs, xr, low, basis_sub, basis_root)
     return new_sub.T, new_root, gram.T
 
 

time: 120 us -> 116 us (0.967)
  local copies, waits for them, and re-layouts: 4.79 us -> 0 us
    unnamed x3 -> x0, local copies, waits for them, and re-layouts: 4.79 us -> none
    pallas_call x0 -> x1, Pallas kernels: none -> 3.29 us  [body(): pl.pallas_call(finish, grid=(NF // STEP,), out_shape=(jax.ShapeDtypeStruc...]
    pallas_call x1, Pallas kernels: 114 us -> 112 us  [body(): pl.pallas_call(kernel, out_shape=(jax.ShapeDtypeStruct((N, SH), F32), jax...]
where the time goes in v3:
time: 116 us
  Pallas kernels  115 us (99%)
    pallas_call x1, Pallas kernels, body(): pl.pallas_call(kernel, out_shape=(jax.ShapeDtypeStruct((N, SH), F32), jax...  112 us
    pallas_call x1, Pallas kernels, body(): pl.pallas_call(finish, grid=(NF // STEP,), out_shape=(jax.ShapeDtypeStruc...  3.29 us

profile of v3, /device:TPU:1, one launch (start us, length us, event | category | flops | bytes accessed | tf_op | source)
XLA Modules:
  0.0 115.8 jit_solution(7808080552994885017)
XLA Ops:
  0.6 111.8 %shard_map.130 = (f32[64,512]{1,0:T(8,128)}, f32[48,64]{1,0:T(8,128)}, bf16[8,4,16,256]{3,2,1,0:T(8,128)(2,1)}) custom-call(f32[64,512]{1,0:T(8,128)} %bitcast.10, f32[48,64]{1,0:T(8,128)} %rroot_hbm.1, bf16[512,4096]{1,0:T(8,128)(2,1)} %bitcast.8, bf16[2048,512]{1,0:T(8,128)(2,1)} %bitcast.9, s32[1,2048]{1,0:T(1,128)} %rows_hbm.1, ...), custom_call_target="tpu_custom_call" | custom-call | tf_op jit(solution)/shard_map/pallas_call | solution.py:603
  112.5 3.3 %shard_map.131 = (f32[64,512]{1,0:T(8,128)}, f32[48,64]{1,0:T(8,128)}, f32[64,2048]{1,0:T(8,128)}) custom-call(f32[64,512]{1,0:T(8,128)} %get-tuple-element.9.xs_ref, f32[48,64]{1,0:T(8,128)} %get-tuple-element.10.xr_ref, bf16[8,4,16,256]{3,2,1,0:T(8,128)(2,1)} %get-tuple-element.11.g_ref, bf16[512,2048]{1,0:T(8,128)(2,1)} %bas_ref.1, bf16[48,2048]{1,0:T(8,128)(2,1)} %brt_ref.1), custom_call_target="tpu_custom_call" | custom-call | tf_op jit(solution)/shard_map/pallas_call | solution.py:681

commit v4 on v3

--- a/solution.py
+++ b/solution.py
@@ -30,7 +30,7 @@
 NB = 2048
 NBS = NB // NF
 PAD = 128
-STEP = 4
+STEP = 8
 ORDER = (4, 5, 3, 2, 6, 7, 1)
 SENDS = 240
 RECVS = 160
@@ -89,6 +89,7 @@
     x_send,
     x_recv,
     x_all,
+    x_sum,
     xr_send,
     xr_recv,
     pk_send,
@@ -121,6 +122,16 @@
     c = lax.rem(f, NC)
     other = 1 - c
 
+    def slice_of(i):
+        half = lax.div(i, NC)
+        return jnp.where(lax.rem(i, NC) == 0, half, NF - 1 - half)
+
+    def holder_of(i):
+        return jnp.where(i < NX, NC * i, NC * (NF - 1 - i) + 1)
+
+    part = slice_of(f)
+    reached = z >= part
+
     def dev_f(i):
         return (g, i)
 
@@ -163,9 +174,6 @@
         load_brt,
         load_bas,
     ) = loads
-    for load in loads:
-        load.start()
-
     barrier = pltpu.get_barrier_semaphore()
     def hops(k, n):
         return min(k, n - k)
@@ -185,30 +193,52 @@
     ]
     for _, dev in sorted(peers, key=lambda peer: -peer[0]):
         pl.semaphore_signal(barrier, inc=1, device_id=dev, device_id_type=MESH)
+    for load in loads:
+        load.start()
 
     sends = []
+    later = []
     slots = [0]
+    sent = [0]
 
     def take(n):
         slots[0] += n
         assert slots[0] <= RECVS
         return slots[0] - n
 
-    def push(src, dst, slot, dev, cond=None):
-        assert len(sends) < SENDS
+    def push(src, dst, slot, dev, cond=None, to=sends):
+        assert sent[0] < SENDS
         copy = pltpu.make_async_remote_copy(
             src_ref=src,
             dst_ref=dst,
-            send_sem=ssem.at[len(sends)],
+            send_sem=ssem.at[sent[0]],
             recv_sem=rsem.at[slot],
             device_id=dev,
             device_id_type=MESH,
         )
+        sent[0] += 1
         if cond is None:
             copy.start()
         else:
             pl.when(cond)(copy.start)
-        sends.append((copy, cond))
+        to.append((copy, cond))
+
+    def settle(keep, of=sends):
+        done = of[: len(of) - keep]
+        del of[: len(of) - keep]
+        while done:
+            cond = done[0][1]
+            same = [copy for copy, other_cond in done if other_cond is cond]
+            done = [pair for pair in done if pair[1] is not cond]
+
+            def wait(same=same):
+                for copy in same:
+                    copy.wait_send()
+
+            if cond is None:
+                wait()
+            else:
+                pl.when(cond)(wait)
 
     def land(buf, slot):
         pltpu.make_async_remote_copy(
@@ -256,13 +286,13 @@
         push(rhs_all.at[f], rhs_all.at[f], at + f, dev_f(turn(f, k, NF)), f + k < NF)
     at_rhs = at
     at_rr = take(NF)
-    push(rr_send, rr_all.at[f], at_rr + f, dev_f(z), f != z)
+    push(rr_send, rr_all.at[f], at_rr + f, dev_f(holder_of(z)), part != z)
 
     load_rows.wait()
 
     def hot(i, _):
         rows = pl.ds(pl.multiple_of(i * 64, 64), 64)
-        ids = lax.broadcasted_iota(jnp.int32, (64, UP), 0) + (f * SL + i * 64)
+        ids = lax.broadcasted_iota(jnp.int32, (64, UP), 0) + (part * SL + i * 64)
         onehot[rows, :] = jnp.where(ids == rows_ref[...], 1.0, 0.0).astype(BF)
         return 0
 
@@ -309,13 +339,14 @@
             push(up_send.at[k], up_recv.at[f], at + f, dev_f(p))
         else:
             up_recv[f] = piece
-
-    @pl.when(f == z)
+    settle(NF - 1)
+
+    @pl.when(part == z)
     def _():
         land_ring(rr_all, at_rr, f, NF)
         rr_sum[...] = sum(dot(rr_all[j], place(j)) for j in range(NF))
 
-    @pl.when(f != z)
+    @pl.when(part != z)
     def _():
         rr_sum[...] = jnp.zeros_like(rr_sum)
 
@@ -331,45 +362,42 @@
     my_rows = pl.ds(pl.multiple_of(f * RR, 16), RR)
     for k in range(1, NF):
         p = turn(f, k, NF)
-        cols = pl.ds(pl.multiple_of(p * SL, 128), SL)
-        push(frs.at[:, cols], frt.at[my_rows], at_frt + f, dev_f(p))
-    frt[my_rows, :] = frs[:, pl.ds(pl.multiple_of(f * SL, 128), SL)]
+        to = slice_of(p)
+        cols = pl.ds(pl.multiple_of(to * SL, 128), SL)
+        push(frs.at[:, cols], frt.at[my_rows], at_frt + f, dev_f(p), to <= z, later)
+    frt[my_rows, :] = frs[:, pl.ds(pl.multiple_of(part * SL, 128), SL)]
 
     adds = lax.rem(z + y + c, 2) == 0
     spot_mine = 2 * z + lax.div(y, 2)
 
-    def leaf_sum(chunk, send, recv, full):
-        at_sum = take(1)
-        at_full = take(1)
-        for turn_q in (2, 1, 3, 0):
-            q = turn(lax.div(z, 2), turn_q, NY)
-            send[q] = chunk(q).astype(BF).reshape(NS, N // NS, GR)
-            for s in range(NS):
-                zi = 2 * q + s // 2
-                to = zi * NY + 2 * (s % 2) + lax.rem(zi + c, 2)
-                slot = lax.rem(g - to + NG - 1, NG)
-                push(send.at[q, s], recv.at[slot], at_sum, (to, f), to != g)
-
-        @pl.when(adds)
-        def _():
-            land(recv.at[pl.ds(0, NG - 1)], at_sum)
-            q = lax.div(spot_mine, NS)
-            total = send[q, lax.rem(spot_mine, NS)].astype(F32)
-            for j in range(NG - 1):
-                total += recv[j].astype(F32)
-            full[spot_mine] = total.astype(BF)
-
+    def cut(chunk, q, send):
+        send[q] = chunk(q).astype(BF).reshape(NS, N // NS, GR)
+
+    def hand_out(q, send, recv, slot_of, at, cond=None):
+        for i in range(NS):
+            zi = 2 * q + i // 2
+            to = zi * NY + 2 * (i % 2) + lax.rem(zi + c, 2)
+            use = to != g if cond is None else cond & (to != g)
+            push(send.at[q, i], recv.at[slot_of(to)], at, (to, f), use)
+
+    def own_piece(send):
+        return send[lax.div(spot_mine, NS), lax.rem(spot_mine, NS)]
+
+    def hand_back(full, some):
+        at = take(1)
         for k in sorted(range(1, NG), key=lambda k: -min(k, NG - k)):
             to = turn(g, k, NG)
-            push(full.at[spot_mine], full.at[spot_mine], at_full, (to, f), adds)
-
-        @pl.when(adds)
+            use = adds & (lax.div(to, NY) >= part) if some else adds
+            push(full.at[spot_mine], full.at[spot_mine], at, (to, f), use)
+        wanted = reached if some else part >= 0
+
+        @pl.when(adds & wanted)
         def _():
-            land(full.at[pl.ds(0, NR - 1)], at_full)
-
-        @pl.when(jnp.logical_not(adds))
+            land(full.at[pl.ds(0, NR - 1)], at)
+
+        @pl.when(jnp.logical_not(adds) & wanted)
         def _():
-            land(full, at_full)
+            land(full, at)
 
         parts = [full[pl.ds(NS * j, NS)].reshape(N, GR) for j in range(NY)]
         return jnp.concatenate(parts, axis=1)
@@ -380,12 +408,34 @@
         total = dot_t(up_low, onehot[pl.ds(pl.multiple_of(q * GR, 128), GR), :])
         return jnp.where(q == y, rr_sum[...], 0.0) - total
 
-    b_low = leaf_sum(scatter_chunk, d_send, d_recv, d_all)
-
-    land_ring_rows = [turn(f, NF - k, NF) for k in range(1, NF)]
-    for p in land_ring_rows:
-        land(frt.at[pl.ds(pl.multiple_of(p * RR, 16), RR)], at_frt + p)
-    yr_send[...] = dot_t(b_low, frt[...]).astype(BF)
+    at = take(1)
+    for k in (2, 1, 3, 0):
+        q = turn(lax.div(z, 2), k, NY)
+        cut(scatter_chunk, q, d_send)
+        hand_out(q, d_send, d_recv, lambda to: lax.rem(g - to + NG - 1, NG), at)
+    settle(NR)
+
+    @pl.when(adds)
+    def _():
+        land(d_recv.at[pl.ds(0, NG - 1)], at)
+        total = own_piece(d_send).astype(F32)
+        for j in range(NG - 1):
+            total += d_recv[j].astype(F32)
+        d_all[spot_mine] = total.astype(BF)
+
+    b_low = hand_back(d_all, True)
+
+    @pl.when(reached)
+    def _():
+        for k in range(1, NF):
+            p = turn(f, NF - k, NF)
+            land(frt.at[pl.ds(pl.multiple_of(p * RR, 16), RR)], at_frt + p)
+        yr_send[...] = dot_t(b_low, frt[...]).astype(BF)
+
+    @pl.when(jnp.logical_not(reached))
+    def _():
+        yr_send[...] = jnp.zeros_like(yr_send)
+
     at = take(1)
     push(yr_send, yr_sib, at, dev_f(x * NC + other))
     land(yr_sib, at)
@@ -393,13 +443,49 @@
     at = take(NX)
     for k in (2, 1, 3):
         push(yr_all.at[x], yr_all.at[x], at + x, dev_x(turn(x, k, NX)))
+    settle(NX - 1)
     land_ring(yr_all, at, x, NX)
     yr_low = sum(yr_all[j].astype(F32) for j in range(NX)).astype(BF)
 
     def back_chunk(q):
         return dot(yr_low, frt[:, pl.ds(pl.multiple_of(q * GR, 128), GR)])
 
-    x_low = leaf_sum(back_chunk, x_send, x_recv, x_all)
+    at = take(NZ)
+    for k in (2, 1, 3, 0):
+        q = turn(lax.div(z, 2), k, NY)
+
+        @pl.when(reached)
+        def _(q=q):
+            cut(back_chunk, q, x_send)
+
+        hand_out(q, x_send, x_recv, lambda to: g, at + z, reached)
+    settle(NR)
+
+    @pl.when(adds)
+    def _():
+        x_sum[...] = jnp.zeros_like(x_sum)
+
+        @pl.when(reached)
+        def _():
+            x_recv[g] = own_piece(x_send)
+
+        for i in range(NZ):
+
+            @pl.when(i >= part)
+            def _(i=i):
+                @pl.when(z == i)
+                def _():
+                    land(x_recv.at[pl.ds(NY * i, NY - 1)], at + i)
+
+                @pl.when(z != i)
+                def _():
+                    land(x_recv.at[pl.ds(NY * i, NY)], at + i)
+
+                x_sum[...] += sum(x_recv[NY * i + j].astype(F32) for j in range(NY))
+
+        x_all[spot_mine] = x_sum[...].astype(BF)
+
+    x_low = hand_back(x_all, False)
 
     at = take(NF)
     for k in ORDER + (0,):
@@ -413,7 +499,7 @@
             pk_recv[f] = piece
     at_xr = take(1)
 
-    @pl.when(f == z)
+    @pl.when(part == z)
     def _():
         block = x_all[pl.ds(pl.multiple_of(NS * y, NS), NS)].reshape(N, GR)
         for j in range(NF):
@@ -422,7 +508,9 @@
 
     for k in ORDER:
         p = turn(f, k, NF)
-        push(xr_send.at[p], xr_recv, at_xr, dev_f(p), f == z)
+        push(xr_send.at[p], xr_recv, at_xr, dev_f(p), part == z)
+    settle(2 * NF - 2)
+    settle(0, later)
     land_ring(pk_recv, at, f, NF)
     pk_all[f] = sum(pk_recv[j].astype(F32) for j in range(NF)).astype(BF)
     at = take(NF)
@@ -487,7 +575,9 @@
     if_send[1] = dot(xs_low[:, :RIM], iface_ref[...]).astype(BF)
     push(if_send.at[1], if_recv.at[1], at_prev, (turn(g, NG - 1, NG), f))
 
-    @pl.when(f != z)
+    settle(2)
+
+    @pl.when(part != z)
     def _():
         land(xr_recv, at_xr)
 
@@ -522,13 +612,14 @@
     for i in (2, 1, 3, 0):
         xi = turn(x, i, NX)
         land(gc_recv.at[xi], at + xi)
-        part = gc_own[xi] + gc_recv[xi].astype(F32)
-        gp_send[xi] = part.astype(BF).reshape(NY, N // NY, NBS)
+        pair = gc_own[xi] + gc_recv[xi].astype(F32)
+        gp_send[xi] = pair.astype(BF).reshape(NY, N // NY, NBS)
         for j in (2, 1, 3, 0):
             if i or j:
                 yj = turn(y, j, NY)
                 slot = ((NX - i) % NX) * NY + (NY - j) % NY - 1
                 push(gp_send.at[xi, yj], gp_recv.at[slot], at_p, dev_xy(xi, yj))
+    settle(NX * NY - 1)
     land(gp_recv, at_p)
     total = gp_send[x, y].astype(F32)
     for j in range(NX * NY - 1):
@@ -537,6 +628,7 @@
     at = take(NZ)
     for k in (4, 3, 5, 2, 6, 1, 7):
         push(gz_all.at[z], gz_all.at[z], at + z, dev_z(turn(z, k, NZ)))
+    settle(NZ - 1)
     land_ring(gz_all, at, z, NZ)
     mine = c * NX + x
     g_all[mine, y] = sum(gz_all[j].astype(F32) for j in range(NZ)).astype(BF)
@@ -546,6 +638,7 @@
             if i or j:
                 to = dev_xy(turn(x, i, NX), turn(y, j, NY))
                 push(g_all.at[mine, y], g_all.at[mine, y], at, to)
+    settle(NX * NY - 1)
     land(gp_recv, at)
     at = take(1)
     half = pl.ds(pl.multiple_of(c * NX, NX), NX)
@@ -553,16 +646,13 @@
 
     keep_mine = pltpu.make_async_copy(g_all.at[half], g_hbm.at[half], lsem.at[13])
     keep_mine.start()
+    settle(1)
     rest = pl.ds(pl.multiple_of(other * NX, NX), NX)
     land(g_all.at[rest], at)
     keep_rest = pltpu.make_async_copy(g_all.at[rest], g_hbm.at[rest], lsem.at[14])
     keep_rest.start()
 
-    for copy, cond in sends:
-        if cond is None:
-            copy.wait_send()
-        else:
-            pl.when(cond)(copy.wait_send)
+    settle(0)
     for keep in (keep_sub, keep_root, keep_mine, keep_rest):
         keep.wait()
 
@@ -636,6 +726,7 @@
             pltpu.VMEM((N, GR), BF),
             pltpu.VMEM((NX, N, GR), BF),
             *leaf_sum,
+            pltpu.VMEM((N // NS, GR), F32),
             pltpu.VMEM((NF, N, PAD), BF),
             pltpu.VMEM((N, PAD), BF),
             pltpu.VMEM((NF, N, UPS), BF),

time: 116 us -> 115 us (level)
  no operation moved by 1% of the time
where the time goes in v4:
time: 115 us
  Pallas kernels  114 us (99%)
    pallas_call x1, Pallas kernels, body(): pl.pallas_call(kernel, out_shape=(jax.ShapeDtypeStruct((N, SH), F32), jax...  111 us
    pallas_call x1, Pallas kernels, body(): pl.pallas_call(finish, grid=(NF // STEP,), out_shape=(jax.ShapeDtypeStruc...  3.34 us

profile of v4, /device:TPU:1, one launch (start us, length us, event | category | flops | bytes accessed | tf_op | source)
XLA Modules:
  0.0 114.8 jit_solution(12841786502452221409)
XLA Ops:
  0.6 110.8 %shard_map.130 = (f32[64,512]{1,0:T(8,128)}, f32[48,64]{1,0:T(8,128)}, bf16[8,4,16,256]{3,2,1,0:T(8,128)(2,1)}) custom-call(f32[64,512]{1,0:T(8,128)} %bitcast.10, f32[48,64]{1,0:T(8,128)} %rroot_hbm.1, bf16[512,4096]{1,0:T(8,128)(2,1)} %bitcast.8, bf16[2048,512]{1,0:T(8,128)(2,1)} %bitcast.9, s32[1,2048]{1,0:T(1,128)} %rows_hbm.1, ...), custom_call_target="tpu_custom_call" | custom-call | tf_op jit(solution)/shard_map/pallas_call | solution.py:693
  111.4 3.3 %shard_map.131 = (f32[64,512]{1,0:T(8,128)}, f32[48,64]{1,0:T(8,128)}, f32[64,2048]{1,0:T(8,128)}) custom-call(f32[64,512]{1,0:T(8,128)} %get-tuple-element.9.xs_ref, f32[48,64]{1,0:T(8,128)} %get-tuple-element.10.xr_ref, bf16[8,4,16,256]{3,2,1,0:T(8,128)(2,1)} %get-tuple-element.11.g_ref, bf16[512,2048]{1,0:T(8,128)(2,1)} %bas_ref.1, bf16[48,2048]{1,0:T(8,128)(2,1)} %brt_ref.1), custom_call_target="tpu_custom_call" | custom-call | tf_op jit(solution)/shard_map/pallas_call | solution.py:772

commit v5 on v4

--- a/solution.py
+++ b/solution.py
@@ -32,8 +32,8 @@
 PAD = 128
 STEP = 8
 ORDER = (4, 5, 3, 2, 6, 7, 1)
-SENDS = 240
-RECVS = 160
+SENDS = 72
+RECVS = 46
 
 
 def dot(a, b):
@@ -199,7 +199,7 @@
     sends = []
     later = []
     slots = [0]
-    sent = [0]
+    free = list(range(SENDS))
 
     def take(n):
         slots[0] += n
@@ -207,29 +207,29 @@
         return slots[0] - n
 
     def push(src, dst, slot, dev, cond=None, to=sends):
-        assert sent[0] < SENDS
+        sem = free.pop(0)
         copy = pltpu.make_async_remote_copy(
             src_ref=src,
             dst_ref=dst,
-            send_sem=ssem.at[sent[0]],
+            send_sem=ssem.at[sem],
             recv_sem=rsem.at[slot],
             device_id=dev,
             device_id_type=MESH,
         )
-        sent[0] += 1
         if cond is None:
             copy.start()
         else:
             pl.when(cond)(copy.start)
-        to.append((copy, cond))
+        to.append((copy, cond, sem))
 
     def settle(keep, of=sends):
         done = of[: len(of) - keep]
         del of[: len(of) - keep]
         while done:
             cond = done[0][1]
-            same = [copy for copy, other_cond in done if other_cond is cond]
-            done = [pair for pair in done if pair[1] is not cond]
+            same = [copy for copy, other_cond, _ in done if other_cond is cond]
+            free.extend(sem for _, other_cond, sem in done if other_cond is cond)
+            done = [entry for entry in done if entry[1] is not cond]
 
             def wait(same=same):
                 for copy in same:
@@ -250,10 +250,8 @@
             device_id_type=MESH,
         ).wait_recv()
 
-    def land_ring(buf, base, me, n):
-        for k in range(1, n):
-            p = turn(me, n - k, n)
-            land(buf.at[p], base + p)
+    def land_others(buf, slot):
+        land(buf.at[pl.ds(0, buf.shape[0] - 1)], slot)
 
     spot = lax.broadcasted_iota(jnp.int32, (PAD, GR), 0)
     lane = lax.broadcasted_iota(jnp.int32, (PAD, GR), 1)
@@ -285,8 +283,8 @@
     for k in range(1, NF):
         push(rhs_all.at[f], rhs_all.at[f], at + f, dev_f(turn(f, k, NF)), f + k < NF)
     at_rhs = at
-    at_rr = take(NF)
-    push(rr_send, rr_all.at[f], at_rr + f, dev_f(holder_of(z)), part != z)
+    at_rr = take(1)
+    push(rr_send, rr_all.at[f], at_rr, dev_f(holder_of(z)), part != z)
 
     load_rows.wait()
 
@@ -329,42 +327,42 @@
     y_low = y_acc[...].astype(BF)
 
     load_cpl.wait()
-    at = take(NF)
+    at = take(1)
     for k in ORDER + (0,):
         p = turn(f, k, NF)
         rows = pl.ds(pl.multiple_of(p * UPS, 128), UPS)
         piece = dot_t(y_low, cpl[rows, :]).astype(BF)
         if k:
             up_send[k] = piece
-            push(up_send.at[k], up_recv.at[f], at + f, dev_f(p))
+            push(up_send.at[k], up_recv.at[f], at, dev_f(p))
         else:
             up_recv[f] = piece
     settle(NF - 1)
 
     @pl.when(part == z)
     def _():
-        land_ring(rr_all, at_rr, f, NF)
+        land_others(rr_all, at_rr)
         rr_sum[...] = sum(dot(rr_all[j], place(j)) for j in range(NF))
 
     @pl.when(part != z)
     def _():
         rr_sum[...] = jnp.zeros_like(rr_sum)
 
-    land_ring(up_recv, at, f, NF)
+    land_others(up_recv, at)
     up_all[f] = sum(up_recv[j].astype(F32) for j in range(NF)).astype(BF)
-    at = take(NF)
+    at = take(1)
     for k in ORDER:
-        push(up_all.at[f], up_all.at[f], at + f, dev_f(turn(f, k, NF)))
-
-    land_ring(up_all, at, f, NF)
-
-    at_frt = take(NF)
+        push(up_all.at[f], up_all.at[f], at, dev_f(turn(f, k, NF)))
+
+    land_others(up_all, at)
+
+    at_frt = take(1)
     my_rows = pl.ds(pl.multiple_of(f * RR, 16), RR)
     for k in range(1, NF):
         p = turn(f, k, NF)
         to = slice_of(p)
         cols = pl.ds(pl.multiple_of(to * SL, 128), SL)
-        push(frs.at[:, cols], frt.at[my_rows], at_frt + f, dev_f(p), to <= z, later)
+        push(frs.at[:, cols], frt.at[my_rows], at_frt, dev_f(p), to <= z, later)
     frt[my_rows, :] = frs[:, pl.ds(pl.multiple_of(part * SL, 128), SL)]
 
     adds = lax.rem(z + y + c, 2) == 0
@@ -427,9 +425,7 @@
 
     @pl.when(reached)
     def _():
-        for k in range(1, NF):
-            p = turn(f, NF - k, NF)
-            land(frt.at[pl.ds(pl.multiple_of(p * RR, 16), RR)], at_frt + p)
+        land(frt.at[pl.ds(0, GR - RR)], at_frt)
         yr_send[...] = dot_t(b_low, frt[...]).astype(BF)
 
     @pl.when(jnp.logical_not(reached))
@@ -440,11 +436,11 @@
     push(yr_send, yr_sib, at, dev_f(x * NC + other))
     land(yr_sib, at)
     yr_all[x] = (yr_send[...].astype(F32) + yr_sib[...].astype(F32)).astype(BF)
-    at = take(NX)
+    at = take(1)
     for k in (2, 1, 3):
-        push(yr_all.at[x], yr_all.at[x], at + x, dev_x(turn(x, k, NX)))
+        push(yr_all.at[x], yr_all.at[x], at, dev_x(turn(x, k, NX)))
     settle(NX - 1)
-    land_ring(yr_all, at, x, NX)
+    land_others(yr_all, at)
     yr_low = sum(yr_all[j].astype(F32) for j in range(NX)).astype(BF)
 
     def back_chunk(q):
@@ -487,14 +483,14 @@
 
     x_low = hand_back(x_all, False)
 
-    at = take(NF)
+    at = take(1)
     for k in ORDER + (0,):
         p = turn(f, k, NF)
         cols = pl.ds(pl.multiple_of(p * UPS, 128), UPS)
         piece = dot(x_low, onehot[:, cols]).astype(BF)
         if k:
             pk_send[k] = piece
-            push(pk_send.at[k], pk_recv.at[f], at + f, dev_f(p))
+            push(pk_send.at[k], pk_recv.at[f], at, dev_f(p))
         else:
             pk_recv[f] = piece
     at_xr = take(1)
@@ -511,15 +507,15 @@
         push(xr_send.at[p], xr_recv, at_xr, dev_f(p), part == z)
     settle(2 * NF - 2)
     settle(0, later)
-    land_ring(pk_recv, at, f, NF)
+    land_others(pk_recv, at)
     pk_all[f] = sum(pk_recv[j].astype(F32) for j in range(NF)).astype(BF)
-    at = take(NF)
+    at = take(1)
     for k in ORDER:
-        push(pk_all.at[f], pk_all.at[f], at + f, dev_f(turn(f, k, NF)))
+        push(pk_all.at[f], pk_all.at[f], at, dev_f(turn(f, k, NF)))
     for k in (0,) + ORDER[::-1]:
         p = turn(f, NF - k, NF)
-        if k:
-            land(pk_all.at[p], at + p)
+        if k == ORDER[-1]:
+            land_others(pk_all, at)
         rows = pl.ds(pl.multiple_of(p * UPS, 128), UPS)
         y_acc[...] -= dot(pk_all[p], cpl[rows, :])
     t_low = y_acc[...].astype(BF)
@@ -625,11 +621,11 @@
     for j in range(NX * NY - 1):
         total += gp_recv[j].astype(F32)
     gz_all[z] = total.astype(BF)
-    at = take(NZ)
+    at = take(1)
     for k in (4, 3, 5, 2, 6, 1, 7):
-        push(gz_all.at[z], gz_all.at[z], at + z, dev_z(turn(z, k, NZ)))
+        push(gz_all.at[z], gz_all.at[z], at, dev_z(turn(z, k, NZ)))
     settle(NZ - 1)
-    land_ring(gz_all, at, z, NZ)
+    land_others(gz_all, at)
     mine = c * NX + x
     g_all[mine, y] = sum(gz_all[j].astype(F32) for j in range(NZ)).astype(BF)
     at = take(1)
@@ -749,7 +745,7 @@
             pltpu.VMEM((NF, NY, N // NY, NBS), BF),
             pltpu.SemaphoreType.DMA((SENDS,)),
             pltpu.SemaphoreType.DMA((RECVS,)),
-            pltpu.SemaphoreType.DMA((16,)),
+            pltpu.SemaphoreType.DMA((15,)),
         ],
         compiler_params=pltpu.CompilerParams(
             collective_id=0, has_side_effects=True, vmem_limit_bytes=56 * 1024 * 1024

time: 115 us -> 112 us (0.974)
  Pallas kernels: 114 us -> 111 us
    pallas_call x1, Pallas kernels: 111 us -> 108 us  [body(): pl.pallas_call(kernel, out_shape=(jax.ShapeDtypeStruct((N, SH), F32), jax...]
where the time goes in v5:
time: 112 us
  Pallas kernels  111 us (99%)
    pallas_call x1, Pallas kernels, body(): pl.pallas_call(kernel, out_shape=(jax.ShapeDtypeStruct((N, SH), F32), jax...  108 us
    pallas_call x1, Pallas kernels, body(): pl.pallas_call(finish, grid=(NF // STEP,), out_shape=(jax.ShapeDtypeStruc...  3.34 us

profile of v5, /device:TPU:1, one launch (start us, length us, event | category | flops | bytes accessed | tf_op | source)
XLA Modules:
  0.0 112.1 jit_solution(18229647190095304265)
XLA Ops:
  0.6 108.1 %shard_map.130 = (f32[64,512]{1,0:T(8,128)}, f32[48,64]{1,0:T(8,128)}, bf16[8,4,16,256]{3,2,1,0:T(8,128)(2,1)}) custom-call(f32[64,512]{1,0:T(8,128)} %bitcast.10, f32[48,64]{1,0:T(8,128)} %rroot_hbm.1, bf16[512,4096]{1,0:T(8,128)(2,1)} %bitcast.8, bf16[2048,512]{1,0:T(8,128)(2,1)} %bitcast.9, s32[1,2048]{1,0:T(1,128)} %rows_hbm.1, ...), custom_call_target="tpu_custom_call" | custom-call | tf_op jit(solution)/shard_map/pallas_call | solution.py:689
  108.8 3.3 %shard_map.131 = (f32[64,512]{1,0:T(8,128)}, f32[48,64]{1,0:T(8,128)}, f32[64,2048]{1,0:T(8,128)}) custom-call(f32[64,512]{1,0:T(8,128)} %get-tuple-element.9.xs_ref, f32[48,64]{1,0:T(8,128)} %get-tuple-element.10.xr_ref, bf16[8,4,16,256]{3,2,1,0:T(8,128)(2,1)} %get-tuple-element.11.g_ref, bf16[512,2048]{1,0:T(8,128)(2,1)} %bas_ref.1, bf16[48,2048]{1,0:T(8,128)(2,1)} %brt_ref.1), custom_call_target="tpu_custom_call" | custom-call | tf_op jit(solution)/shard_map/pallas_call | solution.py:768
